TPU v7x, 256 devices: a whole 4x4x8 slice. The times are simulated.
256 devices in a mesh: wide: 32 (over y, x, core), narrow: 8 (over z).
Axes of the slice: x: 4, y: 4, z: 8, core: 2. Of those that a mesh axis runs over, the one named last changes fastest.
Arguments:
- resid: float32 [4, 2359296], P(None, ('wide', 'narrow')), may hold values from -6 to 6
- mult: int32 [2359296], P(('wide', 'narrow')), may hold values from 1 to 8
- dirichlet_inv: bfloat16 [6144, 384, 384], P(('wide', 'narrow')), may hold values from -0.3125 to 0.3125
- fine_basis: bfloat16 [2359296, 128], P(('wide', 'narrow')), may hold values from -0.1875 to 0.1875
- fine_index: int32 [256, 128], P(('wide', 'narrow')), may hold values from -1 to 511, as said below
- level2_inv: bfloat16 [16384, 512], P('wide'), may hold values from -0.25 to 0.25
- level2_basis: bfloat16 [16384, 128], P('wide'), may hold values from -0.375 to 0.375
- coarse_index: int32 [32, 128], P('wide'), may hold values from 0 to 2047, as said below
- coarse_inv: bfloat16 [2048, 2048], P('wide'), may hold values from -0.25 to 0.25
Outputs:
- correction: float32 [4, 2359296], P(None, ('wide', 'narrow'))
Inputs may be any that keep to these rules, and one draw needn't show every extreme that they name: `fine_index`: row s lists the level-2 positions of fine subdomain s's primal unknowns: at least 64 valid entries from the start, then -1 as padding; entries may repeat. `coarse_index`: entries may repeat within a row.
All inputs are finite; a program needn't handle non-finite values.
Results may differ from a plain program's by a relative error of at most 0.02.
Values may be sent and summed in bfloat16 or wider, within the bound.
No kernel may reach another device: no remote copies, remote signals or barrier semaphores. Data moves between devices by JAX's collectives and lax.ppermute only.
A program may use at most 64 MiB of HBM per device.

v0:
```python
import jax
import jax.numpy as jnp
from jax import lax
from jax.sharding import PartitionSpec as P

NF = 1152


def padded_2(cells, sides, width):
    for axis, dim in sides:
        count = lax.axis_size(axis)
        ends = count - 1
        head = lax.slice_in_dim(cells, 0, width, axis=dim)
        tail = lax.slice_in_dim(cells, cells.shape[dim] - width, cells.shape[dim], axis=dim)
        cells = jnp.concatenate(
            [
                lax.ppermute(tail, axis, [(i, (i + 1) % count) for i in range(ends)]),
                cells,
                lax.ppermute(head, axis, [((i + 1) % count, i) for i in range(ends)]),
            ],
            axis=dim,
        )
    return cells


def per_device(
    resid,
    mult,
    dirichlet_inv,
    fine_basis,
    fine_index,
    level2_inv,
    level2_basis,
    coarse_index,
    coarse_inv,
):
    highest = lax.Precision.HIGHEST
    loads, width = resid.shape
    blocks, block_size = (dirichlet_inv.shape[0], dirichlet_inv.shape[1])
    weights = mult.astype(jnp.float32)[None, :]
    weighted = (resid / weights).astype(jnp.bfloat16)
    interior = jnp.einsum(
        "bij,kbj->kbi",
        dirichlet_inv,
        weighted.reshape(loads, blocks, block_size),
        preferred_element_type=jnp.float32,
    ).reshape(loads, width)
    fine_primal = jnp.dot(weighted, fine_basis, preferred_element_type=jnp.float32)
    level_width = level2_inv.shape[1]
    select = fine_index.reshape(-1, 1) == jnp.arange(level_width, dtype=jnp.int32)[None, :]
    contrib = jnp.dot(fine_primal, select.astype(jnp.float32), precision=highest)
    level2_resid = lax.psum(contrib, "narrow")
    level2_low = level2_resid.astype(jnp.bfloat16)
    level2_local = jnp.einsum(
        "kj,ij->ki", level2_low, level2_inv, preferred_element_type=jnp.float32
    )
    level2_primal = jnp.dot(level2_low, level2_basis, preferred_element_type=jnp.float32)
    coarse_width = coarse_inv.shape[1]
    pick_two = coarse_index.reshape(-1, 1) == jnp.arange(coarse_width, dtype=jnp.int32)[None, :]
    coarse_part = jnp.dot(level2_primal, pick_two.astype(jnp.float32), precision=highest)
    coarse_resid = lax.psum(coarse_part.astype(jnp.bfloat16), "wide")
    own_rows = jnp.einsum(
        "kj,ij->ki", coarse_resid, coarse_inv, preferred_element_type=jnp.float32
    ).astype(jnp.bfloat16)
    coarse_corr = lax.all_gather(own_rows, "wide", axis=1, tiled=True)
    picked = jnp.einsum(
        "kt,ct->kc", coarse_corr, pick_two.astype(jnp.bfloat16), preferred_element_type=jnp.float32
    ).astype(jnp.bfloat16)
    level2_corr = (
        level2_local
        + jnp.einsum("kc,mc->km", picked, level2_basis, preferred_element_type=jnp.float32)
    ).astype(jnp.bfloat16)
    gathered = jnp.einsum(
        "km,pm->kp", level2_corr, select.astype(jnp.bfloat16), preferred_element_type=jnp.float32
    ).astype(jnp.bfloat16)
    fine_corr = interior + jnp.einsum(
        "kp,dp->kd", gathered, fine_basis, preferred_element_type=jnp.float32
    )
    scaled = fine_corr / weights
    padded = padded_2(scaled.astype(jnp.bfloat16), (("wide", 1),), NF).astype(scaled.dtype)
    result = scaled.at[:, :NF].add(padded[:, :NF])
    result = result.at[:, width - NF :].add(padded[:, NF + width :])
    return result


def solution(mesh):
    placed = (
        P(None, ("wide", "narrow")),
        P(("wide", "narrow")),
        P(("wide", "narrow"), None, None),
        P(("wide", "narrow"), None),
        P(("wide", "narrow"), None),
        P("wide", None),
        P("wide", None),
        P("wide", None),
        P("wide", None),
    )
    return jax.shard_map(
        per_device,
        mesh=mesh,
        in_specs=placed,
        out_specs=P(None, ("wide", "narrow")),
        check_vma=False,
    )
```

profile of v0, /device:TPU:1, one launch (start us, length us, event | category | flops | bytes accessed | tf_op | source)
XLA Modules:
  0.0 189.3 jit_solution(1562119067232201049)
XLA Ops:
  0.0 0.0 copy-start
  0.0 0.0 copy-start.6
  0.0 0.0 copy-start.4
  0.0 0.0 copy-start.5
  0.0 0.0 copy-start.2
  0.0 0.0 copy-start.1
  0.0 0.9 convert_element_type.34
  1.0 1.0 divide_convert_fusion
  2.0 0.0 copy-done
  2.0 0.4 fusion.19
  2.4 0.0 copy-done.6
  2.4 0.3 fusion.7
  2.7 17.5 %psum.14 = bf16[4,512]{1,0:T(4,128)(2,1)S(1)} all-reduce(f32[4,512]{1,0:T(4,128)S(1)} %fusion.7), channel_id=1, replica_groups=mesh['wide'=32,'narrow'=8] {'narrow'}, use_global_device_ids=true, to_apply=%region_0.0 | all-reduce | flops 2048 | bytes 12288 | tf_op jit(solution)/shard_map/psum | solution.py:52
  20.2 0.0 copy-done.4
  20.2 0.1 fusion.20
  20.3 0.0 copy-done.5
  20.3 0.5 convolution_convert_fusion
  20.8 123.5 %psum.15 = bf16[4,2048]{1,0:T(4,128)(2,1)S(1)} all-reduce(bf16[4,2048]{1,0:T(4,128)(2,1)S(1)} %convolution_convert_fusion), channel_id=1, replica_groups=mesh['wide'=32,'narrow'=8] {'wide'}, use_global_device_ids=true, to_apply=%region_1.0 | all-reduce | flops 8192 | bytes 32768 | tf_op jit(solution)/shard_map/psum | solution.py:61
  144.3 0.0 copy-done.2
  144.3 0.2 fusion.4
  144.5 25.8 %all-gather = bf16[32,64,4]{1,2,0:T(4,128)(2,1)S(1)} all-gather(bf16[1,64,4]{1,2,0:T(4,128)(2,1)S(1)} %fusion.4), channel_id=1, replica_groups=mesh['wide'=32,'narrow'=8] {'wide'}, dimensions={0}, use_global_device_ids=true | all-gather | bytes 16896 | tf_op jit(solution)/shard_map/all_gather | solution.py:65
  170.3 0.1 reshape.63
  170.4 0.3 convolution_convert_fusion.1
  170.7 0.0 copy-done.1
  170.7 0.2 fusion.21
  171.0 0.3 fusion.3
  171.3 5.2 %fusion.18 = f32[24,4,384]{2,1,0:T(4,128)S(1)} fusion(bf16[4,24,384]{2,0,1:T(4,128)(2,1)S(1)} %bitcast.29, bf16[24,384,384]{2,1,0:T(8,128)(2,1)} %param.15), kind=kOutput, calls=%fused_computation.31 | convolution fusion | flops 28311552 | bytes 7299072 | tf_op jit(solution)/shard_map/bij,kbj->kbi/dot_general | solution.py:42
  176.4 0.7 fusion.17
  177.2 4.5 %collective-permute-start = (bf16[4,1152]{1,0:T(4,128)(2,1)S(1)}, bf16[4,1152]{1,0:T(4,128)(2,1)S(1)}, u32[]{:S(2)}, u32[]{:S(2)}) collective-permute-start(bf16[4,1152]{1,0:T(4,128)(2,1)S(1)} %get-tuple-element.29), channel_id=1, source_target_pairs={{0,8},{8,16},{16,24},{24,32},{32,40},{40,48},{48,56},{56,64},{64,7... | collective-permute-start | bytes 27656 | tf_op jit(solution)/shard_map/ppermute | solution.py:17
  181.7 1.9 %collective-permute-start.1 = (bf16[4,1152]{1,0:T(4,128)(2,1)S(1)}, bf16[4,1152]{1,0:T(4,128)(2,1)S(1)}, u32[]{:S(2)}, u32[]{:S(2)}) collective-permute-start(bf16[4,1152]{1,0:T(4,128)(2,1)S(1)} %get-tuple-element.30), channel_id=1, source_target_pairs={{8,0},{16,8},{24,16},{32,24},{40,32},{48,40},{56,48},{64,56},{72,6... | collective-permute-start | bytes 27656 | tf_op jit(solution)/shard_map/ppermute | solution.py:19
  183.6 0.6 compare_reduce_fusion
  184.2 0.0 collective-permute-done
  184.2 2.4 %collective-permute-done.1 = bf16[4,1152]{1,0:T(4,128)(2,1)S(1)} collective-permute-done((bf16[4,1152]{1,0:T(4,128)(2,1)S(1)}, bf16[4,1152]{1,0:T(4,128)(2,1)S(1)}, u32[]{:S(2)}, u32[]{:S(2)}) %collective-permute-start.1) | collective-permute-done | bytes 9248 | tf_op jit(solution)/shard_map/ppermute | solution.py:19
  186.6 0.7 fusion.10
  187.3 0.0 copy-start.3
  187.3 0.7 copy-done.3
  188.0 1.3 fusion.11
  (2 shorter events, 0.0 us)
Async XLA Ops:
  0.0 2.0 %copy-start = (bf16[9216,128]{1,0:T(8,128)(2,1)S(1)}, bf16[9216,128]{1,0:T(8,128)(2,1)}, u32[]{:S(2)}) copy-start(bf16[9216,128]{1,0:T(8,128)(2,1)} %param.16) | copy-start | bytes 7077892
  0.0 2.4 %copy-start.6 = (s32[1,128]{1,0:T(1,128)S(1)}, s32[1,128]{1,0:T(1,128)}, u32[]{:S(2)}) copy-start(s32[1,128]{1,0:T(1,128)} %param.17) | copy-start | bytes 1540
  0.0 20.2 %copy-start.4 = (bf16[512,128]{1,0:T(8,128)(2,1)S(1)}, bf16[512,128]{1,0:T(8,128)(2,1)}, u32[]{:S(2)}) copy-start(bf16[512,128]{1,0:T(8,128)(2,1)} %param.19) | copy-start | bytes 393220
  0.0 20.3 %copy-start.5 = (s32[1,128]{1,0:T(1,128)S(1)}, s32[1,128]{1,0:T(1,128)}, u32[]{:S(2)}) copy-start(s32[1,128]{1,0:T(1,128)} %param.20) | copy-start | bytes 1540
  0.0 144.3 %copy-start.2 = (bf16[64,2048]{1,0:T(8,128)(2,1)S(1)}, bf16[64,2048]{1,0:T(8,128)(2,1)}, u32[]{:S(2)}) copy-start(bf16[64,2048]{1,0:T(8,128)(2,1)} %param.21) | copy-start | bytes 786436
  0.0 170.7 %copy-start.1 = (bf16[512,512]{1,0:T(8,128)(2,1)S(1)}, bf16[512,512]{1,0:T(8,128)(2,1)}, u32[]{:S(2)}) copy-start(bf16[512,512]{1,0:T(8,128)(2,1)} %param.18) | copy-start | bytes 1572868
  177.2 7.0 %collective-permute-start = (bf16[4,1152]{1,0:T(4,128)(2,1)S(1)}, bf16[4,1152]{1,0:T(4,128)(2,1)S(1)}, u32[]{:S(2)}, u32[]{:S(2)}) collective-permute-start(bf16[4,1152]{1,0:T(4,128)(2,1)S(1)} %get-tuple-element.29), channel_id=1, source_target_pairs={{0,8},{8,16},{16,24},{24,32},{32,40},{40,48},{48,56},{56,64},{64,7... | collective-permute-start | bytes 27656 | tf_op jit(solution)/shard_map/ppermute | solution.py:17
  181.7 5.0 %collective-permute-start.1 = (bf16[4,1152]{1,0:T(4,128)(2,1)S(1)}, bf16[4,1152]{1,0:T(4,128)(2,1)S(1)}, u32[]{:S(2)}, u32[]{:S(2)}) collective-permute-start(bf16[4,1152]{1,0:T(4,128)(2,1)S(1)} %get-tuple-element.30), channel_id=1, source_target_pairs={{8,0},{16,8},{24,16},{32,24},{40,32},{48,40},{56,48},{64,56},{72,6... | collective-permute-start | bytes 27656 | tf_op jit(solution)/shard_map/ppermute | solution.py:19
  187.3 0.7 copy-start.3
where the time goes:
time: 191 us; the launch traced here: 189 us
  blocking collectives  167 us (87%)
  matrix products  8.25 us (4%)
  starting transfers between devices  6.37 us (3%)
  other arithmetic  4.59 us (2%)
  waiting for transfers between devices  2.41 us (1%)
    psum x1, blocking collectives, per_device(): coarse_resid = lax.psum(coarse_part.astype(jnp.bfloat16), 'wide')  123 us
    all_gather x1, blocking collectives, per_device(): coarse_corr = lax.all_gather(own_rows, 'wide', axis=1, tiled=True)  25.8 us
    psum x1, blocking collectives, per_device(): level2_resid = lax.psum(contrib, 'narrow')  17.5 us
    dot_general x1, matrix products, per_device(): jnp.einsum('bij,kbj->kbi', dirichlet_inv, weighted.reshape(loads, blocks,...  5.17 us
    ppermute x1, starting transfers between devices, padded_2(): lax.ppermute(tail, axis, [(i, (i + 1) % count) for i in range(ends)])  4.45 us
  transfers between devices with their start and end apart: 2, of which 1 were waited for; matrix products, arithmetic and copies ran while one was open for 0% of the time, Pallas kernels for 0%

commit v1 on v0

v1 whole, which is shorter than its diff:
```python
import jax
import jax.numpy as jnp
from jax import lax
from jax.sharding import PartitionSpec as P

NF = 1152


def spread(chunk, axis):
    count = lax.axis_size(axis)
    return lax.all_to_all(jnp.broadcast_to(chunk[None], (count,) + chunk.shape), axis, 0, 0)


def per_device(
    resid,
    mult,
    dirichlet_inv,
    fine_basis,
    fine_index,
    level2_inv,
    level2_basis,
    coarse_index,
    coarse_inv,
):
    f32, bf16 = jnp.float32, jnp.bfloat16
    highest = lax.Precision.HIGHEST
    loads, width = resid.shape
    blocks, block_size = dirichlet_inv.shape[0], dirichlet_inv.shape[1]
    level_width = level2_inv.shape[1]
    coarse_width = coarse_inv.shape[1]
    rows = coarse_inv.shape[0]
    count = lax.axis_size("wide")

    inverse = (1.0 / mult.astype(f32))[None, :]
    weighted = (resid * inverse).astype(bf16)
    fine_primal = jnp.dot(weighted, fine_basis, preferred_element_type=f32)
    select = fine_index.reshape(-1, 1) == jnp.arange(level_width, dtype=jnp.int32)[None, :]
    contrib = jnp.dot(fine_primal, select.astype(f32), precision=highest)

    level2_low = jnp.sum(spread(contrib, "narrow"), axis=0).astype(bf16)
    interior = jnp.einsum(
        "bij,kbj->kbi",
        dirichlet_inv,
        weighted.reshape(loads, blocks, block_size),
        preferred_element_type=f32,
    ).reshape(loads, width)
    level2_local = jnp.einsum("kj,ij->ki", level2_low, level2_inv, preferred_element_type=f32)
    level2_primal = jnp.dot(level2_low, level2_basis, preferred_element_type=f32)

    own_high = coarse_index // 128
    own_low = coarse_index % 128
    packet = jnp.concatenate(
        [level2_primal.astype(bf16), own_high.astype(bf16), own_low.astype(bf16), jnp.zeros((2, 128), bf16)], axis=0
    )
    packets = spread(packet, "wide")
    high = packets[:, loads : loads + 1, :]
    low = packets[:, loads + 1, :].reshape(1, -1)
    tall = jnp.concatenate(
        [jnp.where(high == jnp.asarray(h, bf16), packets[:, :loads], jnp.zeros((), bf16)) for h in range(coarse_width // 128)],
        axis=1,
    )
    tall = jnp.swapaxes(tall, 0, 1).reshape(-1, count * 128)
    one_hot = (low == jnp.arange(128, dtype=bf16)[:, None]).astype(bf16)
    coarse_resid = lax.dot_general(tall, one_hot, (((1,), (1,)), ((), ())), preferred_element_type=f32)
    coarse_low = jnp.swapaxes(coarse_resid.reshape(-1, loads, 128), 0, 1).reshape(loads, coarse_width).astype(bf16)
    own_rows = jnp.einsum("kj,ij->ki", coarse_low, coarse_inv, preferred_element_type=f32).astype(bf16)

    corr = spread(own_rows, "wide")
    pick_low = (coarse_index % rows == jnp.arange(rows, dtype=jnp.int32)[:, None]).astype(bf16)
    picks = jnp.dot(corr.reshape(count * loads, rows), pick_low, preferred_element_type=f32)
    mask = (coarse_index // rows)[None] == jnp.arange(count, dtype=jnp.int32)[:, None, None]
    picked = jnp.sum(jnp.where(mask, picks.reshape(count, loads, 128), 0.0), axis=0).astype(bf16)
    level2_corr = (
        level2_local + jnp.einsum("kc,mc->km", picked, level2_basis, preferred_element_type=f32)
    ).astype(bf16)
    gathered = jnp.einsum(
        "km,pm->kp", level2_corr, select.astype(bf16), preferred_element_type=f32
    ).astype(bf16)
    scaled = (
        interior + jnp.einsum("kp,dp->kd", gathered, fine_basis, preferred_element_type=f32)
    ) * inverse

    head = scaled[:, :NF].astype(bf16)
    tail = scaled[:, width - NF :].astype(bf16)
    even = lax.axis_index("wide") % 2 == 0
    near = [(i, i ^ 1) for i in range(count)]
    far = [(i, ((i + 1) ^ 1) - 1) for i in range(1, count - 1)]
    from_near = lax.ppermute(jnp.where(even, tail, head), "wide", near)
    from_far = lax.ppermute(jnp.where(even, head, tail), "wide", far)
    to_head = jnp.where(even, from_far, from_near).astype(f32)
    to_tail = jnp.where(even, from_near, from_far).astype(f32)
    return jnp.concatenate(
        [scaled[:, :NF] + to_head, scaled[:, NF : width - NF], scaled[:, width - NF :] + to_tail], axis=1
    )


def solution(mesh):
    placed = (
        P(None, ("wide", "narrow")),
        P(("wide", "narrow")),
        P(("wide", "narrow"), None, None),
        P(("wide", "narrow"), None),
        P(("wide", "narrow"), None),
        P("wide", None),
        P("wide", None),
        P("wide", None),
        P("wide", None),
    )
    return jax.shard_map(
        per_device,
        mesh=mesh,
        in_specs=placed,
        out_specs=P(None, ("wide", "narrow")),
        check_vma=False,
    )
```

time: 191 us -> 61.6 us (0.32)
  blocking collectives: 167 us -> 0 us
  starting transfers between devices: 6.37 us -> 24.9 us
  waiting for transfers between devices: 2.41 us -> 16 us
  local copies, waits for them, and re-layouts: 0.81 us -> 5.24 us
  matrix products: 8.25 us -> 10.2 us
    psum x2 -> x0, blocking collectives: 141 us -> none  [the longest x1 123 us: per_device(): coarse_resid = lax.psum(coarse_part.astype(jnp.bfloat16), 'wide')]
    all_gather x1 -> x0, blocking collectives: 25.8 us -> none  [per_device(): coarse_corr = lax.all_gather(own_rows, 'wide', axis=1, tiled=True)]
    all_to_all x0 -> x3, starting transfers between devices: none -> 22.1 us  [spread(): lax.all_to_all(jnp.broadcast_to(chunk[None], (count,) + chunk.shape), axi...]
    all_to_all x0 -> x3, waiting for transfers between devices: none -> 13.9 us  [spread(): lax.all_to_all(jnp.broadcast_to(chunk[None], (count,) + chunk.shape), axi...]
    ppermute x2, starting transfers between devices: 6.37 us -> 2.84 us  [the longest x1 2.75 us: per_device(): from_far = lax.ppermute(jnp.where(even, head, tail), 'wide', far)]
    scatter-add x2 -> x0, other arithmetic: 1.99 us -> none  [the longest x1 1.33 us: per_device(): result = result.at[:, width - NF:].add(padded[:, NF + width:])]
    dot_general x9, matrix products: 3.08 us -> 5.03 us  [the longest x1 1.28 us: per_device(): jnp.einsum('kj,ij->ki', level2_low, level2_inv, preferred_element_type=f32)]
  transfers between devices with their start and end apart: 2 -> 5, of which waited for: 1 -> 4; matrix products, arithmetic and copies ran while one was open for 0% -> 13% of each run, Pallas kernels for 0% -> 0%
where the time goes in v1:
time: 61.6 us; the launch traced here: 60.9 us
  starting transfers between devices  24.9 us (40%)
  waiting for transfers between devices  16 us (26%)
  matrix products  10.2 us (17%)
  local copies, waits for them, and re-layouts  5.24 us (9%)
  other arithmetic  4.34 us (7%)
    all_to_all x3, starting transfers between devices, spread(): lax.all_to_all(jnp.broadcast_to(chunk[None], (count,) + chunk.shape), axi...  22.1 us
    all_to_all x3, waiting for transfers between devices, spread(): lax.all_to_all(jnp.broadcast_to(chunk[None], (count,) + chunk.shape), axi...  13.9 us
    dot_general x1, matrix products, per_device(): jnp.einsum('bij,kbj->kbi', dirichlet_inv, weighted.reshape(loads, blocks,...  5.16 us
    ppermute x1, starting transfers between devices, per_device(): from_far = lax.ppermute(jnp.where(even, head, tail), 'wide', far)  2.75 us
    unnamed x25, local copies, waits for them, and re-layouts  2.21 us
    ppermute x1, waiting for transfers between devices, per_device(): from_far = lax.ppermute(jnp.where(even, head, tail), 'wide', far)  2.11 us
    broadcast_in_dim x3, local copies, waits for them, and re-layouts, spread(): jnp.broadcast_to(chunk[None], (count,) + chunk.shape)  1.31 us
    dot_general x1, matrix products, per_device(): jnp.einsum('kj,ij->ki', level2_low, level2_inv, preferred_element_type=f32)  1.28 us
  transfers between devices with their start and end apart: 5, of which 4 were waited for; matrix products, arithmetic and copies ran while one was open for 13% of the time, Pallas kernels for 0%

profile of v1, /device:TPU:1, one launch (start us, length us, event | category | flops | bytes accessed | tf_op | source)
XLA Modules:
  0.0 60.9 jit_solution(4865973855216663716)
XLA Ops:
  0.0 0.0 copy-start
  0.0 0.9 %convert_divide_fusion = f32[9216]{0:T(1024)S(1)} fusion(s32[9216]{0:T(1024)} %param.10), kind=kLoop, calls=%fused_computation.24 | loop fusion | flops 18432 | bytes 73728 | tf_op jit(solution)/shard_map/div | solution.py:34
  0.9 0.0 copy-start.1
  0.9 0.6 copy-done.1
  1.5 1.0 %multiply_convert_fusion = bf16[4,9216]{1,0:T(4,128)(2,1)S(1)} fusion(f32[4,9216]{1,0:T(4,128)} %param.9, f32[9216]{0:T(1024)S(1)} %convert_divide_fusion), kind=kLoop, calls=%fused_computation.21 | loop fusion | flops 73728 | bytes 258048 | tf_op jit(solution)/shard_map/convert_element_type | solution.py:35
  2.5 0.0 copy-done
  2.5 0.4 fusion.37
  2.9 0.0 copy-done.9
  2.9 0.3 fusion.17
  3.2 0.6 %broadcast_in_dim.173 = f32[8,4,512]{2,1,0:T(4,128)} broadcast(f32[4,512]{1,0:T(4,128)S(1)} %fusion.17), dimensions={1,2} | broadcast | bytes 73728 | tf_op jit(solution)/shard_map/broadcast_in_dim | solution.py:11
  3.8 9.0 %all-to-all-start = ((f32[8,4,512]{2,1,0:T(4,128)}), f32[8,4,512]{2,1,0:T(4,128)S(1)}, u32[]{:S(2)}, u32[]{:S(2)}) async-start(f32[8,4,512]{2,1,0:T(4,128)} %broadcast_in_dim.173), calls=%async_computation | async-start | bytes 131072 | tf_op jit(solution)/shard_map/all_to_all | solution.py:11
  12.9 0.1 pad.6.clone
  12.9 5.2 %fusion.36 = f32[24,4,384]{2,1,0:T(4,128)S(1)} fusion(bf16[4,24,384]{2,0,1:T(4,128)(2,1)S(1)} %bitcast.76, bf16[24,384,384]{2,1,0:T(8,128)(2,1)} %param.11), kind=kOutput, calls=%fused_computation.91 | convolution fusion | flops 28311552 | bytes 7299072 | tf_op jit(solution)/shard_map/bij,kbj->kbi/dot_general | solution.py:41
  18.1 0.0 copy-done.7
  18.1 0.5 fusion.32
  18.6 1.4 %all-to-all-done = f32[8,4,512]{2,1,0:T(4,128)S(1)} async-done(((f32[8,4,512]{2,1,0:T(4,128)}), f32[8,4,512]{2,1,0:T(4,128)S(1)}, u32[]{:S(2)}, u32[]{:S(2)}) %all-to-all-start) | async-done | bytes 65568 | tf_op jit(solution)/shard_map/all_to_all | solution.py:11
  20.1 0.1 convolution_convert_fusion.1
  20.3 0.1 maximum_maximum_fusion
  20.3 0.6 %broadcast_in_dim.176 = bf16[32,8,128]{2,1,0:T(8,128)(2,1)} broadcast(bf16[8,128]{1,0:T(8,128)(2,1)S(1)} %maximum_maximum_fusion), dimensions={1,2} | broadcast | bytes 67584 | tf_op jit(solution)/shard_map/broadcast_in_dim | solution.py:11
  21.0 9.2 %all-to-all-start.1 = ((bf16[32,8,128]{2,1,0:T(8,128)(2,1)}), bf16[32,8,128]{2,1,0:T(8,128)(2,1)S(1)}, u32[]{:S(2)}, u32[]{:S(2)}) async-start(bf16[32,8,128]{2,1,0:T(8,128)(2,1)} %broadcast_in_dim.176), calls=%async_computation.1 | async-start | bytes 131072 | tf_op jit(solution)/shard_map/all_to_all | solution.py:11
  30.2 0.6 iota_compare_fusion.4
  30.8 6.7 %all-to-all-done.1 = bf16[32,8,128]{2,1,0:T(8,128)(2,1)S(1)} async-done(((bf16[32,8,128]{2,1,0:T(8,128)(2,1)}), bf16[32,8,128]{2,1,0:T(8,128)(2,1)S(1)}, u32[]{:S(2)}, u32[]{:S(2)}) %all-to-all-start.1) | async-done | bytes 65568 | tf_op jit(solution)/shard_map/all_to_all | solution.py:11
  37.5 0.6 %fusion.35 = (bf16[32,1,128]{2,1,0:T(2,128)(2,1)}, bf16[32,1,128]{2,1,0:T(2,128)(2,1)S(1)}) fusion(bf16[32,8,128]{2,1,0:T(8,128)(2,1)S(1)} %all-to-all-done.1), kind=kLoop, calls=%fused_computation.90 | loop fusion | bytes 32768 | tf_op jit(solution)/shard_map/slice | solution.py:57
  38.2 0.2 broadcast_select_fusion.1
  38.4 0.2 broadcast_select_fusion
  38.7 0.5 concatenate.10
  39.2 0.3 copy.33
  39.5 0.1 dot_general.40
  39.7 0.0 copy-start.4
  39.7 0.0 copy-start.10
  39.7 0.8 %copy.51 = bf16[32,1,128]{2,0,1:T(8,128)(2,1)S(1)} copy(bf16[32,1,128]{2,1,0:T(2,128)(2,1)} %get-tuple-element.11) | data formatting | bytes 16384
  40.5 0.7 %fusion.8 = bf16[1,4,16,128]{3,2,1,0:T(8,128)(2,1)S(1)} fusion(bf16[16,4,4096]{2,1,0:T(4,128)(2,1)S(1)} %dot_general.40, bf16[4096]{0:T(1024)(128)(2,1)S(1)} %bitcast.78), kind=kOutput, calls=%fused_computation.8 | convolution fusion | flops 68689920 | bytes 548864 | tf_op jit(solution)/shard_map/dot_general | solution.py:64
  41.2 1.1 %convolution_convert_fusion = bf16[4,64]{1,0:T(4,128)(2,1)S(1)} fusion(bf16[64,2048]{1,0:T(8,128)(2,1)} %param.17, bf16[1,4,16,128]{3,2,1,0:T(8,128)(2,1)S(1)} %fusion.8), kind=kOutput, calls=%fused_computation.13 | convolution fusion | flops 1048832 | bytes 279040 | tf_op jit(solution)/shard_map/kj,ij->ki/dot_general | solution.py:66
  42.3 0.7 %reshape.50 = bf16[32,2,128]{2,1,0:T(2,128)(2,1)} reshape(bf16[32,4,64]{2,1,0:T(4,128)(2,1)S(1)} %broadcast_in_dim.210) | data formatting | bytes 32768
  43.0 3.9 %all-to-all-start.2 = ((bf16[32,2,128]{2,1,0:T(2,128)(2,1)}), bf16[32,2,128]{2,1,0:T(2,128)(2,1)S(1)}, u32[]{:S(2)}, u32[]{:S(2)}) async-start(bf16[32,2,128]{2,1,0:T(2,128)(2,1)} %reshape.50), calls=%async_computation.2 | async-start | bytes 32768 | tf_op jit(solution)/shard_map/all_to_all | solution.py:11
  46.9 1.3 %fusion.38 = f32[4,512]{1,0:T(4,128)S(1)} fusion(bf16[4,512]{1,0:T(4,128)(2,1)} %copy-done.5, bf16[512,512]{1,0:T(8,128)(2,1)} %param.14), kind=kOutput, calls=%fused_computation.93 | convolution fusion | flops 2097152 | bytes 536576 | tf_op jit(solution)/shard_map/kj,ij->ki/dot_general | solution.py:47
  48.2 5.7 %all-to-all-done.2 = bf16[32,2,128]{2,1,0:T(2,128)(2,1)S(1)} async-done(((bf16[32,2,128]{2,1,0:T(2,128)(2,1)}), bf16[32,2,128]{2,1,0:T(2,128)(2,1)S(1)}, u32[]{:S(2)}, u32[]{:S(2)}) %all-to-all-start.2) | async-done | bytes 16416 | tf_op jit(solution)/shard_map/all_to_all | solution.py:11
  53.9 0.1 reshape.51
  54.0 0.0 copy-done.6
  54.0 0.2 fusion.4
  54.1 0.3 fusion.13
  54.4 0.0 copy-done.2
  54.4 0.7 %fusion = f32[4,9216]{1,0:T(4,128)S(1)} fusion(f32[4,9216]{1,0:T(4,128)S(1)} %bitcast.77, bf16[4,128]{1,0:T(4,128)(2,1)S(1)} %fusion.13, bf16[9216,128]{1,0:T(8,128)(2,1)S(1)} %copy-done, f32[9216]{0:T(1024)S(1)} %copy-done.2), kind=kOutput, calls=%fused_computation.1 | convolution fusion | flops 9510912 | bytes 2692096 | tf_op jit(solution)/shard_map/kp,dp->kd/dot_general | solution.py:80
  55.2 2.7 %collective-permute-start = (bf16[4,1152]{1,0:T(4,128)(2,1)S(1)}, bf16[4,1152]{1,0:T(4,128)(2,1)S(1)}, u32[]{:S(2)}, u32[]{:S(2)}) collective-permute-start(bf16[4,1152]{1,0:T(4,128)(2,1)S(1)} %get-tuple-element.9), channel_id=1, source_target_pairs={{8,16},{16,8},{24,32},{32,24},{40,48},{48,40},{56,64},{64,56},{72,... | collective-permute-start | bytes 27656 | tf_op jit(solution)/shard_map/ppermute | solution.py:89
  57.9 0.1 collective-permute-start.1
  58.1 2.1 %collective-permute-done = bf16[4,1152]{1,0:T(4,128)(2,1)S(1)} collective-permute-done((bf16[4,1152]{1,0:T(4,128)(2,1)S(1)}, bf16[4,1152]{1,0:T(4,128)(2,1)S(1)}, u32[]{:S(2)}, u32[]{:S(2)}) %collective-permute-start) | collective-permute-done | bytes 9248 | tf_op jit(solution)/shard_map/ppermute | solution.py:89
  60.2 0.0 collective-permute-done.1
  60.2 0.7 %pad_maximum_fusion = f32[4,9216]{1,0:T(4,128)} fusion(f32[4,1152]{1,0:T(4,128)S(1)} %get-tuple-element.8, f32[4,6912]{1,0:T(4,128)S(1)} %slice.46, f32[4,1152]{1,0:T(4,128)S(1)} %get-tuple-element.7), kind=kLoop, calls=%fused_computation.20 | loop fusion | flops 73728 | bytes 294912 | tf_op jit(solution)/shard_map/concatenate | solution.py:92
  (20 shorter events, 0.2 us)
Async XLA Ops:
  0.0 2.5 %copy-start = (bf16[9216,128]{1,0:T(8,128)(2,1)S(1)}, bf16[9216,128]{1,0:T(8,128)(2,1)}, u32[]{:S(2)}) copy-start(bf16[9216,128]{1,0:T(8,128)(2,1)} %param.12) | copy-start | bytes 7077892
  0.0 2.9 %copy-start.9 = (s32[1,128]{1,0:T(1,128)S(1)}, s32[1,128]{1,0:T(1,128)}, u32[]{:S(2)}) copy-start(s32[1,128]{1,0:T(1,128)} %param.13) | copy-start | bytes 1540
  0.9 0.6 copy-start.1
  3.8 16.3 %all-to-all-start = ((f32[8,4,512]{2,1,0:T(4,128)}), f32[8,4,512]{2,1,0:T(4,128)S(1)}, u32[]{:S(2)}, u32[]{:S(2)}) async-start(f32[8,4,512]{2,1,0:T(4,128)} %broadcast_in_dim.173), calls=%async_computation | async-start | bytes 131072 | tf_op jit(solution)/shard_map/all_to_all | solution.py:11
  12.9 5.2 %copy-start.7 = (s32[1,128]{1,0:T(1,128)S(1)}, s32[1,128]{1,0:T(1,128)}, u32[]{:S(2)}) copy-start(s32[1,128]{1,0:T(1,128)} %param.16) | copy-start | bytes 1540
  12.9 7.2 %copy-start.3 = (bf16[512,128]{1,0:T(8,128)(2,1)S(1)}, bf16[512,128]{1,0:T(8,128)(2,1)}, u32[]{:S(2)}) copy-start(bf16[512,128]{1,0:T(8,128)(2,1)} %param.15) | copy-start | bytes 393220
  20.1 0.9 %copy-start.5 = (bf16[4,512]{1,0:T(4,128)(2,1)}, bf16[4,512]{1,0:T(4,128)(2,1)S(1)}, u32[]{:S(2)}) copy-start(bf16[4,512]{1,0:T(4,128)(2,1)S(1)} %reduce_sum.18) | copy-start | bytes 12292
  21.0 16.5 %all-to-all-start.1 = ((bf16[32,8,128]{2,1,0:T(8,128)(2,1)}), bf16[32,8,128]{2,1,0:T(8,128)(2,1)S(1)}, u32[]{:S(2)}, u32[]{:S(2)}) async-start(bf16[32,8,128]{2,1,0:T(8,128)(2,1)} %broadcast_in_dim.176), calls=%async_computation.1 | async-start | bytes 131072 | tf_op jit(solution)/shard_map/all_to_all | solution.py:11
  39.7 14.3 %copy-start.6 = (pred[32,128]{1,0:T(8,128)(4,1)S(1)}, pred[32,128]{1,0:T(8,128)(4,1)}, u32[]{:S(2)}) copy-start(pred[32,128]{1,0:T(8,128)(4,1)} %iota_compare_fusion.4) | copy-start | bytes 12292
  39.7 14.3 %copy-start.8 = (s32[128]{0:T(128)S(1)}, s32[128]{0:T(128)}, u32[]{:S(2)}) copy-start(s32[128]{0:T(128)} %get-tuple-element.44) | copy-start | bytes 1540
  39.7 14.4 %copy-start.4 = (bf16[512,128]{1,0:T(8,128)(2,1)S(1)}, bf16[512,128]{1,0:T(8,128)(2,1)}, u32[]{:S(2)}) copy-start(bf16[512,128]{1,0:T(8,128)(2,1)} %param.15) | copy-start | bytes 393220
  39.7 14.4 %copy-start.10 = (s32[1,128]{1,0:T(1,128)S(1)}, s32[1,128]{1,0:T(1,128)}, u32[]{:S(2)}) copy-start(s32[1,128]{1,0:T(1,128)} %param.13) | copy-start | bytes 1540
  39.7 14.7 %copy-start.2 = (f32[9216]{0:T(1024)S(1)}, f32[9216]{0:T(1024)}, u32[]{:S(2)}) copy-start(f32[9216]{0:T(1024)} %copy-done.1) | copy-start | bytes 110596
  43.0 10.9 %all-to-all-start.2 = ((bf16[32,2,128]{2,1,0:T(2,128)(2,1)}), bf16[32,2,128]{2,1,0:T(2,128)(2,1)S(1)}, u32[]{:S(2)}, u32[]{:S(2)}) async-start(bf16[32,2,128]{2,1,0:T(2,128)(2,1)} %reshape.50), calls=%async_computation.2 | async-start | bytes 32768 | tf_op jit(solution)/shard_map/all_to_all | solution.py:11
  55.2 5.0 %collective-permute-start = (bf16[4,1152]{1,0:T(4,128)(2,1)S(1)}, bf16[4,1152]{1,0:T(4,128)(2,1)S(1)}, u32[]{:S(2)}, u32[]{:S(2)}) collective-permute-start(bf16[4,1152]{1,0:T(4,128)(2,1)S(1)} %get-tuple-element.9), channel_id=1, source_target_pairs={{8,16},{16,8},{24,32},{32,24},{40,48},{48,40},{56,64},{64,56},{72,... | collective-permute-start | bytes 27656 | tf_op jit(solution)/shard_map/ppermute | solution.py:89
  57.9 2.2 %collective-permute-start.1 = (bf16[4,1152]{1,0:T(4,128)(2,1)S(1)}, bf16[4,1152]{1,0:T(4,128)(2,1)S(1)}, u32[]{:S(2)}, u32[]{:S(2)}) collective-permute-start(bf16[4,1152]{1,0:T(4,128)(2,1)S(1)} %get-tuple-element.10), channel_id=1, source_target_pairs={{0,8},{8,0},{16,24},{24,16},{32,40},{40,32},{48,56},{56,48},{64,72... | collective-permute-start | bytes 27656 | tf_op jit(solution)/shard_map/ppermute | solution.py:88

commit v2 on v0

v2 whole, which is shorter than its diff:
```python
import functools

import jax
import jax.numpy as jnp
from jax import lax
from jax.experimental import pallas as pl
from jax.experimental.pallas import tpu as pltpu
from jax.sharding import PartitionSpec as P

NF = 1152
LANES = 128
F32 = jnp.float32
BF16 = jnp.bfloat16
LIMIT = 16 * 1024 * 1024
NN = (((1,), (0,)), ((), ()))
NT = (((1,), (1,)), ((), ()))
VMEM = pl.BlockSpec(memory_space=pltpu.VMEM)


def mm(a, b, dims=NN):
    return lax.dot_general(a, b, dims, preferred_element_type=F32)


def split_mm(a, b, dims=NN):
    high = a.astype(BF16)
    rest = a - high.astype(F32)
    mid = rest.astype(BF16)
    low = (rest - mid.astype(F32)).astype(BF16)
    return mm(high, b, dims) + (mm(mid, b, dims) + mm(low, b, dims))


def selector(index_row, width):
    column = jnp.transpose(jnp.broadcast_to(index_row.astype(F32), (LANES, LANES)))
    lane = lax.broadcasted_iota(jnp.int32, (LANES, LANES), 1).astype(F32)
    return jnp.concatenate(
        [jnp.where(column == lane + float(q * LANES), 1.0, 0.0) for q in range(width // LANES)], axis=1
    ).astype(BF16)


def sides(width):
    me = lax.axis_index("wide")
    odd = lax.rem(me, 2)
    last = width - NF
    near = me + 1 - 2 * odd
    far = jnp.clip(me - 1 + 2 * odd, 0, lax.axis_size("wide") - 1)
    return (pl.multiple_of(last * (1 - odd), LANES), near), (pl.multiple_of(last * odd, LANES), far)


def copies_of(pairs, sems):
    copies = [pltpu.make_async_copy(source, target, sems.at[at]) for at, (source, target) in enumerate(pairs)]
    for copy in copies:
        copy.start()
    return copies


def head_kernel(
    resid_hbm,
    mult_hbm,
    basis_hbm,
    index_hbm,
    basis_ref,
    weighted_ref,
    weight_ref,
    inverse_ref,
    send_ref,
    resid_ref,
    mult_ref,
    index_ref,
    sems,
):
    width = resid_ref.shape[1]
    level_width = 4 * LANES
    parts = sems.shape[0] - 3
    step = width // parts
    cuts = [slice(part * step, (part + 1) * step) for part in range(parts)]
    copies = copies_of(
        [(mult_hbm, mult_ref), (resid_hbm, resid_ref), (index_hbm, index_ref)]
        + [(basis_hbm.at[cut], basis_ref.at[cut]) for cut in cuts],
        sems,
    )
    copies[0].wait()
    weight = mult_ref[...].astype(F32)
    weight_ref[...] = weight
    inverse = 1.0 / weight
    inverse_ref[...] = inverse
    copies[1].wait()
    weighted = (resid_ref[...] * inverse).astype(BF16)
    weighted_ref[...] = weighted
    copies[2].wait()
    select = selector(index_ref[...], level_width)
    total = jnp.zeros((resid_ref.shape[0], LANES), F32)
    for part, cut in enumerate(cuts):
        copies[3 + part].wait()
        total += mm(weighted[:, cut], basis_ref[cut, :])
    contrib = split_mm(total, select)
    chunk = jnp.concatenate(
        [contrib[:, q * LANES : (q + 1) * LANES] for q in range(level_width // LANES)], axis=0
    ).astype(BF16)
    for other in range(send_ref.shape[0]):
        send_ref[other] = chunk


def interior_kernel(weighted_ref, blocks_hbm, interior_ref, blocks_ref, sems, *, depth):
    count, size = blocks_ref.shape[0], blocks_ref.shape[1]

    def copy(b):
        return pltpu.make_async_copy(blocks_hbm.at[b], blocks_ref.at[b], sems.at[b])

    for b in range(depth):
        copy(b).start()
    for b in range(count):
        copy(b).wait()
        if b + depth < count:
            copy(b + depth).start()
        cut = slice(b * size, (b + 1) * size)
        interior_ref[:, cut] = mm(weighted_ref[:, cut], blocks_ref[b], NT)


def level2_kernel(
    parts_ref,
    inverse_ref,
    level2_basis_ref,
    index_ref,
    coarse_index_ref,
    interior_ref,
    weight_ref,
    basis_ref,
    local_ref,
    send_ref,
    picked_ref,
    near_ref,
    far_ref,
    packet,
    stage,
):
    loads, width = interior_ref.shape
    total = jnp.sum(parts_ref[...].astype(F32), axis=0)
    low = jnp.concatenate([total[q * loads : (q + 1) * loads] for q in range(total.shape[0] // loads)], axis=1).astype(BF16)
    local = mm(low, inverse_ref[...], NT)
    select = selector(index_ref[...], level2_basis_ref.shape[0])
    chosen = mm(select, level2_basis_ref[...]).astype(BF16)
    picked_ref[...] = chosen
    local_picked = split_mm(local, select, NT)
    coarse = coarse_index_ref[...]
    packet[...] = jnp.zeros_like(packet)
    packet[:loads, :] = mm(low, level2_basis_ref[...])
    packet[loads : 2 * loads, :] = local_picked
    packet[8:9, :] = (coarse // LANES).astype(F32)
    packet[9:10, :] = (coarse % LANES).astype(F32)
    local_ref[...] = packet[...]
    chunk = packet[...].astype(BF16)
    for other in range(send_ref.shape[0]):
        send_ref[other] = chunk

    pieces = NF // LANES
    for out_ref, (start, _) in zip((near_ref, far_ref), sides(width)):
        out_ref[:NF, :] = basis_ref[pl.ds(start, NF), :]
        out_ref[NF : NF + LANES, :] = chosen
        stage[loads * pieces :, :] = jnp.zeros((stage.shape[0] - loads * pieces, LANES), F32)
        for q in range(pieces):
            lanes = pl.ds(pl.multiple_of(start + q * LANES, LANES), LANES)
            stage[q * loads : (q + 1) * loads, :] = interior_ref[:, lanes]
            stage[loads * pieces + q : loads * pieces + q + 1, :] = weight_ref[:, lanes]
        out_ref[NF + LANES :, :] = stage[...].astype(BF16)


def coarse_kernel(packets_ref, inverse_ref, coarse_index_ref, send_ref, hot_ref, owner_ref, *, width):
    groups = packets_ref.shape[0]
    half = inverse_ref.shape[0]
    highs = inverse_ref.shape[1] // LANES
    row = lax.broadcasted_iota(jnp.int32, (LANES, LANES), 0).astype(F32)
    tall, hot = [], []
    for g in range(groups):
        packet = packets_ref[g].astype(F32)
        values = packet[:8]
        high = jnp.broadcast_to(packet[8:9], (8, LANES))
        tall.append(jnp.concatenate([jnp.where(high == float(h), values, 0.0) for h in range(highs)], axis=0).astype(BF16))
        hot.append(jnp.where(row == jnp.broadcast_to(packet[9:10], (LANES, LANES)), 1.0, 0.0).astype(BF16))
    total = mm(jnp.concatenate(tall, axis=1), jnp.concatenate(hot, axis=1), NT)
    coarse_low = jnp.concatenate([total[8 * h : 8 * h + 8] for h in range(highs)], axis=1).astype(BF16)
    own = mm(coarse_low, inverse_ref[...], NT)
    own = jnp.concatenate([own, jnp.zeros((8, LANES - half), F32)], axis=1)
    chunk = jnp.concatenate([own, jnp.zeros((8, LANES), F32)], axis=0).astype(BF16)
    for other in range(groups):
        send_ref[other] = chunk

    packets = [packets_ref[group].astype(F32) for _, group in sides(width)]
    places = [coarse_index_ref[...].astype(F32)] + [p[8:9] * float(LANES) + p[9:10] for p in packets]
    place = jnp.concatenate(places, axis=1).astype(jnp.int32)
    shape = (LANES, place.shape[1])
    lane = lax.broadcasted_iota(jnp.int32, shape, 0)
    hot_ref[...] = jnp.where(lane == jnp.broadcast_to(place % half, shape), 1.0, 0.0).astype(BF16)
    owner_ref[...] = jnp.broadcast_to(place // half, owner_ref.shape)


def tail_kernel(
    corr_ref,
    packets_ref,
    hot_ref,
    owner_ref,
    local_ref,
    picked_ref,
    near_ref,
    far_ref,
    interior_ref,
    inverse_ref,
    basis_ref,
    out_hbm,
    out_ref,
    sems,
):
    loads, width = interior_ref.shape
    groups = corr_ref.shape[0]
    table = jnp.concatenate([corr_ref[g].astype(F32)[:8] for g in range(groups)], axis=0).astype(BF16)
    picks = mm(table, hot_ref[...])
    owner = owner_ref[...]
    picked = jnp.zeros(owner.shape, F32)
    for g in range(groups):
        picked += jnp.where(owner == g, picks[8 * g : 8 * g + 8], 0.0)
    picked = picked.astype(BF16)
    gathered = (local_ref[4:8, :] + mm(picked[:, :LANES], picked_ref[...], NT)[:loads]).astype(BF16)

    def piece(cut):
        out_ref[:, cut] = (interior_ref[:, cut] + mm(gathered, basis_ref[cut, :], NT)) * inverse_ref[:, cut]

    def send(cut, at):
        copy = pltpu.make_async_copy(out_ref.at[:, cut], out_hbm.at[:, cut], sems.at[at])
        copy.start()
        return copy

    copies = []
    middle = width - 2 * NF
    step = middle // 2
    for at in range(2):
        cut = slice(NF + at * step, NF + (at + 1) * step)
        piece(cut)
        copies.append(send(cut, at))
    ends = [slice(0, NF), slice(width - NF, width)]
    for cut in ends:
        piece(cut)
    pieces = NF // LANES
    for side, (face_ref, (start, group)) in enumerate(zip((near_ref, far_ref), sides(width))):
        lanes = slice((side + 1) * LANES, (side + 2) * LANES)
        packet = packets_ref[group].astype(F32)
        theirs = (packet[4:8] + mm(picked[:, lanes], face_ref[NF : NF + LANES, :], NT)[:loads]).astype(BF16)
        shift = mm(theirs, face_ref[:NF, :], NT)
        rest = face_ref[NF + LANES :, :].astype(F32)
        weight = rest[loads * pieces : loads * pieces + pieces]
        scale = jnp.where(weight > 0.0, 1.0 / jnp.maximum(weight, 1.0), 0.0)
        for q in range(pieces):
            face = (rest[q * loads : (q + 1) * loads] + shift[:, q * LANES : (q + 1) * LANES]) * scale[q : q + 1]
            at = pl.ds(pl.multiple_of(start + q * LANES, LANES), LANES)
            out_ref[:, at] = out_ref[:, at] + face
    for at, cut in enumerate(ends):
        copies.append(send(cut, 2 + at))
    for copy in copies:
        copy.wait()


def params(limit=LIMIT):
    return pltpu.CompilerParams(vmem_limit_bytes=limit)


def per_device(
    resid,
    mult,
    dirichlet_inv,
    fine_basis,
    fine_index,
    level2_inv,
    level2_basis,
    coarse_index,
    coarse_inv,
):
    loads, width = resid.shape
    blocks, size = dirichlet_inv.shape[0], dirichlet_inv.shape[1]
    wide, narrow = lax.axis_size("wide"), lax.axis_size("narrow")
    mult = mult.reshape(1, width)
    rest_rows = 48

    pieces = 4
    hbm = pl.BlockSpec(memory_space=pltpu.HBM)

    def pinned(*arrays):
        return [pltpu.with_memory_space_constraint(array, pltpu.HBM) for array in arrays]

    basis, weighted, weight, inverse, send = pl.pallas_call(
        head_kernel,
        out_shape=(
            jax.ShapeDtypeStruct(fine_basis.shape, BF16),
            jax.ShapeDtypeStruct((loads, width), BF16),
            jax.ShapeDtypeStruct((1, width), F32),
            jax.ShapeDtypeStruct((1, width), F32),
            jax.ShapeDtypeStruct((narrow, 16, LANES), BF16),
        ),
        in_specs=[hbm] * 4,
        out_specs=(VMEM,) * 5,
        scratch_shapes=[
            pltpu.VMEM(resid.shape, F32),
            pltpu.VMEM(mult.shape, jnp.int32),
            pltpu.VMEM(fine_index.shape, jnp.int32),
            pltpu.SemaphoreType.DMA((3 + pieces,)),
        ],
        compiler_params=params(),
        name="head",
    )(*pinned(resid, mult, fine_basis, fine_index))
    parts = lax.all_to_all(send, "narrow", 0, 0)
    interior = pl.pallas_call(
        functools.partial(interior_kernel, depth=8),
        out_shape=jax.ShapeDtypeStruct((loads, width), F32),
        in_specs=[VMEM, hbm],
        out_specs=VMEM,
        scratch_shapes=[pltpu.VMEM(dirichlet_inv.shape, BF16), pltpu.SemaphoreType.DMA((blocks,))],
        compiler_params=params(),
        cost_estimate=pl.CostEstimate(flops=2 * 16 * blocks * size * size, bytes_accessed=2 * blocks * size * size, transcendentals=0),
        name="interior",
    )(weighted, *pinned(dirichlet_inv))

    face_shape = jax.ShapeDtypeStruct((NF + LANES + rest_rows, LANES), BF16)
    local, send, chosen, near, far = pl.pallas_call(
        level2_kernel,
        out_shape=(
            jax.ShapeDtypeStruct((16, LANES), F32),
            jax.ShapeDtypeStruct((wide, 16, LANES), BF16),
            jax.ShapeDtypeStruct((LANES, LANES), BF16),
            face_shape,
            face_shape,
        ),
        in_specs=[VMEM] * 8,
        out_specs=(VMEM,) * 5,
        scratch_shapes=[pltpu.VMEM((16, LANES), F32), pltpu.VMEM((rest_rows, LANES), F32)],
        compiler_params=params(),
        name="level2",
    )(parts, level2_inv, level2_basis, fine_index, coarse_index, interior, weight, basis)
    near = lax.ppermute(near, "wide", [(i, i ^ 1) for i in range(wide)])
    far = lax.ppermute(far, "wide", [(i, ((i + 1) ^ 1) - 1) for i in range(1, wide - 1)])
    packets = lax.all_to_all(send, "wide", 0, 0)

    send, hot, owner = pl.pallas_call(
        functools.partial(coarse_kernel, width=width),
        out_shape=(
            jax.ShapeDtypeStruct((wide, 16, LANES), BF16),
            jax.ShapeDtypeStruct((LANES, 3 * LANES), BF16),
            jax.ShapeDtypeStruct((8, 3 * LANES), jnp.int32),
        ),
        in_specs=[VMEM] * 3,
        out_specs=(VMEM,) * 3,
        compiler_params=params(),
        name="coarse",
    )(packets, coarse_inv, coarse_index)
    corr = lax.all_to_all(send, "wide", 0, 0)

    return pl.pallas_call(
        tail_kernel,
        out_shape=jax.ShapeDtypeStruct((loads, width), F32),
        in_specs=[VMEM] * 11,
        out_specs=hbm,
        scratch_shapes=[pltpu.VMEM((loads, width), F32), pltpu.SemaphoreType.DMA((4,))],
        compiler_params=params(),
        name="tail",
    )(corr, packets, hot, owner, local, chosen, near, far, interior, inverse, basis)


def solution(mesh):
    placed = (
        P(None, ("wide", "narrow")),
        P(("wide", "narrow")),
        P(("wide", "narrow"), None, None),
        P(("wide", "narrow"), None),
        P(("wide", "narrow"), None),
        P("wide", None),
        P("wide", None),
        P("wide", None),
        P("wide", None),
    )
    return jax.shard_map(
        per_device,
        mesh=mesh,
        in_specs=placed,
        out_specs=P(None, ("wide", "narrow")),
        check_vma=False,
    )
```

time: 191 us -> 53.4 us (0.28)
  blocking collectives: 167 us -> 25.6 us
  Pallas kernels: 0 us -> 12.8 us
  matrix products: 8.25 us -> 0 us
  starting transfers between devices: 6.37 us -> 14.2 us
  other arithmetic: 4.59 us -> 0 us
  waiting for transfers between devices: 2.41 us -> 0.32 us
    psum x2 -> x0, blocking collectives: 141 us -> none  [the longest x1 123 us: per_device(): coarse_resid = lax.psum(coarse_part.astype(jnp.bfloat16), 'wide')]
    all_gather x1 -> x0, blocking collectives: 25.8 us -> none  [per_device(): coarse_corr = lax.all_gather(own_rows, 'wide', axis=1, tiled=True)]
    all_to_all x0 -> x2, blocking collectives: none -> 25.6 us  [the longest x1 14.3 us: per_device(): packets = lax.all_to_all(send, 'wide', 0, 0)]
    pallas_call x0 -> x5, Pallas kernels: none -> 12.8 us  [the longest x1 6.5 us: per_device(): pl.pallas_call(functools.partial(interior_kernel, depth=8), out_shape=jax...]
    all_to_all x0 -> x1, starting transfers between devices: none -> 9.03 us  [per_device(): parts = lax.all_to_all(send, 'narrow', 0, 0)]
    dot_general x10 -> x0, matrix products: 8.25 us -> none  [the longest x1 5.17 us: per_device(): jnp.einsum('bij,kbj->kbi', dirichlet_inv, weighted.reshape(loads, blocks,...]
    ppermute x2, waiting for transfers between devices: 2.41 us -> 0.01 us  [the longest x1 0.01 us: per_device(): near = lax.ppermute(near, 'wide', [(i, i ^ 1) for i in range(wide)])]
    scatter-add x2 -> x0, other arithmetic: 1.99 us -> none  [the longest x1 1.33 us: per_device(): result = result.at[:, width - NF:].add(padded[:, NF + width:])]
  transfers between devices with their start and end apart: 2 -> 3, of which waited for: 1 -> 1; matrix products, arithmetic and copies ran while one was open for 0% -> 0% of each run, Pallas kernels for 0% -> 14%
where the time goes in v2:
time: 53.4 us; the launch traced here: 53.1 us
  blocking collectives  25.6 us (48%)
  starting transfers between devices  14.2 us (27%)
  Pallas kernels  12.8 us (24%)
    all_to_all x1, blocking collectives, per_device(): packets = lax.all_to_all(send, 'wide', 0, 0)  14.3 us
    all_to_all x1, blocking collectives, per_device(): corr = lax.all_to_all(send, 'wide', 0, 0)  11.3 us
    all_to_all x1, starting transfers between devices, per_device(): parts = lax.all_to_all(send, 'narrow', 0, 0)  9.03 us
    pallas_call x1, Pallas kernels, per_device(): pl.pallas_call(functools.partial(interior_kernel, depth=8), out_shape=jax...  6.5 us
    ppermute x1, starting transfers between devices, per_device(): lax.ppermute(far, 'wide', [(i, (i + 1 ^ 1) - 1) for i in range(1, wide -...  3.02 us
    pallas_call x1, Pallas kernels, per_device(): pl.pallas_call(head_kernel, out_shape=(jax.ShapeDtypeStruct(fine_basis.sh...  2.87 us
    ppermute x1, starting transfers between devices, per_device(): near = lax.ppermute(near, 'wide', [(i, i ^ 1) for i in range(wide)])  2.19 us
    pallas_call x1, Pallas kernels, per_device(): pl.pallas_call(tail_kernel, out_shape=jax.ShapeDtypeStruct((loads, width)...  2.11 us
  transfers between devices with their start and end apart: 3, of which 1 were waited for; matrix products, arithmetic and copies ran while one was open for 0% of the time, Pallas kernels for 14%

profile of v2, /device:TPU:1, one launch (start us, length us, event | category | flops | bytes accessed | tf_op | source)
XLA Modules:
  0.0 53.1 jit_solution(5765918219680209524)
XLA Ops:
  0.0 2.9 %head.1 = (bf16[9216,128]{1,0:T(8,128)(2,1)S(1)}, bf16[4,9216]{1,0:T(4,128)(2,1)S(1)}, f32[1,9216]{1,0:T(1,128)S(1)}, f32[1,9216]{1,0:T(1,128)S(1)}, bf16[8,16,128]{2,1,0:T(8,128)(2,1)}) custom-call(f32[4,9216]{1,0:T(4,128)} %resid_hbm.1, s32[1,9216]{1,0:T(1,128)} %bitcast.1, bf16[9216,128]{1,0:T(8,128)(2,1)} %basis_hbm.1, s32[1,128]{1,0:T(1,128)} %index_ref.1), custom_call_target="tpu_custom_call" | custom-call | tf_op jit(solution)/shard_map/head/pallas_call | solution.py:287
  2.9 9.0 %all-to-all-start = ((bf16[8,16,128]{2,1,0:T(8,128)(2,1)}), bf16[8,16,128]{2,1,0:T(8,128)(2,1)S(1)}, u32[]{:S(2)}, u32[]{:S(2)}) async-start(bf16[8,16,128]{2,1,0:T(8,128)(2,1)} %get-tuple-element.18), calls=%async_computation | async-start | bytes 65536 | tf_op jit(solution)/shard_map/all_to_all | solution.py:307
  11.9 0.0 copy-start
  11.9 0.0 copy-start.2
  11.9 0.0 copy-start.3
  11.9 0.0 copy-start.4
  11.9 6.5 %interior.1.interior_ref = f32[4,9216]{1,0:T(4,128)S(1)} custom-call(bf16[4,9216]{1,0:T(4,128)(2,1)S(1)} %get-tuple-element.19.weighted_ref, bf16[24,384,384]{2,1,0:T(8,128)(2,1)} %blocks_hbm.1), custom_call_target="tpu_custom_call" | custom-call | flops 113246208 | bytes 7077888 | tf_op jit(solution)/shard_map/interior/pallas_call | solution.py:308
  18.5 0.0 copy-start.1
  18.5 0.3 all-to-all-done.parts_ref
  18.8 0.0 copy-done
  18.8 0.0 copy-done.2
  18.8 0.0 copy-done.3
  18.8 0.0 copy-done.4
  18.8 0.6 %level2.1 = (f32[16,128]{1,0:T(8,128)S(1)}, bf16[32,16,128]{2,1,0:T(8,128)(2,1)S(1)}, bf16[128,128]{1,0:T(8,128)(2,1)S(1)}, bf16[1328,128]{1,0:T(8,128)(2,1)S(1)}, bf16[1328,128]{1,0:T(8,128)(2,1)S(1)}) custom-call(bf16[8,16,128]{2,1,0:T(8,128)(2,1)S(1)} %all-to-all-done.parts_ref, bf16[512,512]{1,0:T(8,128)(2,1)S(1)} %copy-done, ...), custom_call_target="tpu_custom_call" | custom-call | tf_op jit(solution)/shard_map/level2/pallas_call | solution.py:320
  19.4 2.2 %collective-permute-start = (bf16[1328,128]{1,0:T(8,128)(2,1)S(1)}, bf16[1328,128]{1,0:T(8,128)(2,1)S(1)}, u32[]{:S(2)}, u32[]{:S(2)}) collective-permute-start(bf16[1328,128]{1,0:T(8,128)(2,1)S(1)} %get-tuple-element.28), channel_id=1, source_target_pairs={{0,8},{8,0},{16,24},{24,16},{32,40},{40,32},{48,56},{56,48},{64,72... | collective-permute-start | bytes 1019912 | tf_op jit(solution)/shard_map/ppermute | solution.py:335
  21.6 3.0 %collective-permute-start.1 = (bf16[1328,128]{1,0:T(8,128)(2,1)S(1)}, bf16[1328,128]{1,0:T(8,128)(2,1)S(1)}, u32[]{:S(2)}, u32[]{:S(2)}) collective-permute-start(bf16[1328,128]{1,0:T(8,128)(2,1)S(1)} %get-tuple-element.29), channel_id=1, source_target_pairs={{8,16},{16,8},{24,32},{32,24},{40,48},{48,40},{56,64},{64,56},{72,... | collective-permute-start | bytes 1019912 | tf_op jit(solution)/shard_map/ppermute | solution.py:336
  24.6 14.3 %all_to_all.15.packets_ref = bf16[32,16,128]{2,1,0:T(8,128)(2,1)S(1)} all-to-all(bf16[32,16,128]{2,1,0:T(8,128)(2,1)S(1)} %get-tuple-element.22), channel_id=1, replica_groups=mesh['wide'=32,'narrow'=8] {'wide'}, dimensions={0} | all-to-all | bytes 262144 | tf_op jit(solution)/shard_map/all_to_all | solution.py:337
  39.0 0.0 copy-done.1
  39.0 0.7 %coarse.1 = (bf16[32,16,128]{2,1,0:T(8,128)(2,1)S(1)}, bf16[128,384]{1,0:T(8,128)(2,1)S(1)}, s32[8,384]{1,0:T(8,128)S(1)}) custom-call(bf16[32,16,128]{2,1,0:T(8,128)(2,1)S(1)} %all_to_all.15.packets_ref, bf16[64,2048]{1,0:T(8,128)(2,1)S(1)} %copy-done.1, s32[1,128]{1,0:T(1,128)S(1)} %copy-done.3), custom_call_target="tpu_custom_call" | custom-call | tf_op jit(solution)/shard_map/coarse/pallas_call | solution.py:339
  39.7 11.3 %all_to_all.16.corr_ref = bf16[32,16,128]{2,1,0:T(8,128)(2,1)S(1)} all-to-all(bf16[32,16,128]{2,1,0:T(8,128)(2,1)S(1)} %get-tuple-element.23), channel_id=1, replica_groups=mesh['wide'=32,'narrow'=8] {'wide'}, dimensions={0} | all-to-all | bytes 262144 | tf_op jit(solution)/shard_map/all_to_all | solution.py:351
  51.0 0.0 collective-permute-done.near_ref
  51.0 0.0 collective-permute-done.1.far_ref
  51.0 2.1 %tail.1 = f32[4,9216]{1,0:T(4,128)} custom-call(bf16[32,16,128]{2,1,0:T(8,128)(2,1)S(1)} %all_to_all.16.corr_ref, bf16[32,16,128]{2,1,0:T(8,128)(2,1)S(1)} %all_to_all.15.packets_ref, bf16[128,384]{1,0:T(8,128)(2,1)S(1)} %get-tuple-element.24.hot_ref, s32[8,384]{1,0:T(8,128)S(1)} %get-tuple-element.25.owner_ref, f32[16,128]{1,0:T(8,128)S(1)} %get-tuple-element.26.local_ref, ...), custom_call_target="tpu_custom_call" | custom-call | tf_op jit(solution)/shard_map/tail/pallas_call | solution.py:353
Async XLA Ops:
  2.9 15.9 %all-to-all-start = ((bf16[8,16,128]{2,1,0:T(8,128)(2,1)}), bf16[8,16,128]{2,1,0:T(8,128)(2,1)S(1)}, u32[]{:S(2)}, u32[]{:S(2)}) async-start(bf16[8,16,128]{2,1,0:T(8,128)(2,1)} %get-tuple-element.18), calls=%async_computation | async-start | bytes 65536 | tf_op jit(solution)/shard_map/all_to_all | solution.py:307
  11.9 6.9 %copy-start = (bf16[512,512]{1,0:T(8,128)(2,1)S(1)}, bf16[512,512]{1,0:T(8,128)(2,1)}, u32[]{:S(2)}) copy-start(bf16[512,512]{1,0:T(8,128)(2,1)} %inverse_ref.2) | copy-start | bytes 1572868
  11.9 6.9 %copy-start.2 = (bf16[512,128]{1,0:T(8,128)(2,1)S(1)}, bf16[512,128]{1,0:T(8,128)(2,1)}, u32[]{:S(2)}) copy-start(bf16[512,128]{1,0:T(8,128)(2,1)} %level2_basis_ref.1) | copy-start | bytes 393220
  11.9 6.9 %copy-start.3 = (s32[1,128]{1,0:T(1,128)S(1)}, s32[1,128]{1,0:T(1,128)}, u32[]{:S(2)}) copy-start(s32[1,128]{1,0:T(1,128)} %coarse_index_ref.3) | copy-start | bytes 1540
  11.9 6.9 %copy-start.4 = (s32[1,128]{1,0:T(1,128)S(1)}, s32[1,128]{1,0:T(1,128)}, u32[]{:S(2)}) copy-start(s32[1,128]{1,0:T(1,128)} %index_ref.1) | copy-start | bytes 1540
  18.5 20.5 %copy-start.1 = (bf16[64,2048]{1,0:T(8,128)(2,1)S(1)}, bf16[64,2048]{1,0:T(8,128)(2,1)}, u32[]{:S(2)}) copy-start(bf16[64,2048]{1,0:T(8,128)(2,1)} %inverse_ref.3) | copy-start | bytes 786436
  19.4 31.6 %collective-permute-start = (bf16[1328,128]{1,0:T(8,128)(2,1)S(1)}, bf16[1328,128]{1,0:T(8,128)(2,1)S(1)}, u32[]{:S(2)}, u32[]{:S(2)}) collective-permute-start(bf16[1328,128]{1,0:T(8,128)(2,1)S(1)} %get-tuple-element.28), channel_id=1, source_target_pairs={{0,8},{8,0},{16,24},{24,16},{32,40},{40,32},{48,56},{56,48},{64,72... | collective-permute-start | bytes 1019912 | tf_op jit(solution)/shard_map/ppermute | solution.py:335
  21.6 29.4 %collective-permute-start.1 = (bf16[1328,128]{1,0:T(8,128)(2,1)S(1)}, bf16[1328,128]{1,0:T(8,128)(2,1)S(1)}, u32[]{:S(2)}, u32[]{:S(2)}) collective-permute-start(bf16[1328,128]{1,0:T(8,128)(2,1)S(1)} %get-tuple-element.29), channel_id=1, source_target_pairs={{8,16},{16,8},{24,32},{32,24},{40,48},{48,40},{56,64},{64,56},{72,... | collective-permute-start | bytes 1019912 | tf_op jit(solution)/shard_map/ppermute | solution.py:336

commit v3 on v2

--- a/solution.py
+++ b/solution.py
@@ -38,12 +38,15 @@
 
 
 def sides(width):
-    me = lax.axis_index("wide")
+    me, count = lax.axis_index("wide"), lax.axis_size("wide")
     odd = lax.rem(me, 2)
     last = width - NF
-    near = me + 1 - 2 * odd
-    far = jnp.clip(me - 1 + 2 * odd, 0, lax.axis_size("wide") - 1)
-    return (pl.multiple_of(last * (1 - odd), LANES), near), (pl.multiple_of(last * odd, LANES), far)
+    far = me - 1 + 2 * odd
+    inside = jnp.logical_and(far >= 0, far < count)
+    return (
+        (pl.multiple_of(last * (1 - odd), LANES), me + 1 - 2 * odd, None),
+        (pl.multiple_of(last * odd, LANES), jnp.clip(far, 0, count - 1), inside),
+    )
 
 
 def copies_of(pairs, sems):
@@ -100,20 +103,15 @@
         send_ref[other] = chunk
 
 
-def interior_kernel(weighted_ref, blocks_hbm, interior_ref, blocks_ref, sems, *, depth):
-    count, size = blocks_ref.shape[0], blocks_ref.shape[1]
-
-    def copy(b):
-        return pltpu.make_async_copy(blocks_hbm.at[b], blocks_ref.at[b], sems.at[b])
-
-    for b in range(depth):
-        copy(b).start()
-    for b in range(count):
-        copy(b).wait()
-        if b + depth < count:
-            copy(b + depth).start()
-        cut = slice(b * size, (b + 1) * size)
-        interior_ref[:, cut] = mm(weighted_ref[:, cut], blocks_ref[b], NT)
+def interior_kernel(weighted_ref, blocks_hbm, interior_ref, blocks_ref, sems, *, spans):
+    size = blocks_ref.shape[1]
+    cuts = [pl.ds(first, blocks) for first, blocks in spans]
+    copies = copies_of([(blocks_hbm.at[cut], blocks_ref.at[cut]) for cut in cuts], sems)
+    for copy, (first, blocks) in zip(copies, spans):
+        copy.wait()
+        for b in range(first, first + blocks):
+            cut = slice(b * size, (b + 1) * size)
+            interior_ref[:, cut] = mm(weighted_ref[:, cut], blocks_ref[b], NT)
 
 
 def level2_kernel(
@@ -153,7 +151,7 @@
         send_ref[other] = chunk
 
     pieces = NF // LANES
-    for out_ref, (start, _) in zip((near_ref, far_ref), sides(width)):
+    for out_ref, (start, _, _) in zip((near_ref, far_ref), sides(width)):
         out_ref[:NF, :] = basis_ref[pl.ds(start, NF), :]
         out_ref[NF : NF + LANES, :] = chosen
         stage[loads * pieces :, :] = jnp.zeros((stage.shape[0] - loads * pieces, LANES), F32)
@@ -184,7 +182,7 @@
     for other in range(groups):
         send_ref[other] = chunk
 
-    packets = [packets_ref[group].astype(F32) for _, group in sides(width)]
+    packets = [packets_ref[group].astype(F32) for _, group, _ in sides(width)]
     places = [coarse_index_ref[...].astype(F32)] + [p[8:9] * float(LANES) + p[9:10] for p in packets]
     place = jnp.concatenate(places, axis=1).astype(jnp.int32)
     shape = (LANES, place.shape[1])
@@ -239,14 +237,16 @@
     for cut in ends:
         piece(cut)
     pieces = NF // LANES
-    for side, (face_ref, (start, group)) in enumerate(zip((near_ref, far_ref), sides(width))):
+    for side, (face_ref, (start, group, exists)) in enumerate(zip((near_ref, far_ref), sides(width))):
         lanes = slice((side + 1) * LANES, (side + 2) * LANES)
         packet = packets_ref[group].astype(F32)
         theirs = (packet[4:8] + mm(picked[:, lanes], face_ref[NF : NF + LANES, :], NT)[:loads]).astype(BF16)
         shift = mm(theirs, face_ref[:NF, :], NT)
         rest = face_ref[NF + LANES :, :].astype(F32)
         weight = rest[loads * pieces : loads * pieces + pieces]
-        scale = jnp.where(weight > 0.0, 1.0 / jnp.maximum(weight, 1.0), 0.0)
+        scale = 1.0 / weight
+        if exists is not None:
+            scale = jnp.where(exists, scale, 0.0)
         for q in range(pieces):
             face = (rest[q * loads : (q + 1) * loads] + shift[:, q * LANES : (q + 1) * LANES]) * scale[q : q + 1]
             at = pl.ds(pl.multiple_of(start + q * LANES, LANES), LANES)
@@ -305,12 +305,14 @@
         name="head",
     )(*pinned(resid, mult, fine_basis, fine_index))
     parts = lax.all_to_all(send, "narrow", 0, 0)
+    quarter = blocks // 4
+    spans = tuple((at, quarter) for at in range(0, blocks, quarter))
     interior = pl.pallas_call(
-        functools.partial(interior_kernel, depth=8),
+        functools.partial(interior_kernel, spans=spans),
         out_shape=jax.ShapeDtypeStruct((loads, width), F32),
         in_specs=[VMEM, hbm],
         out_specs=VMEM,
-        scratch_shapes=[pltpu.VMEM(dirichlet_inv.shape, BF16), pltpu.SemaphoreType.DMA((blocks,))],
+        scratch_shapes=[pltpu.VMEM(dirichlet_inv.shape, BF16), pltpu.SemaphoreType.DMA((len(spans),))],
         compiler_params=params(),
         cost_estimate=pl.CostEstimate(flops=2 * 16 * blocks * size * size, bytes_accessed=2 * blocks * size * size, transcendentals=0),
         name="interior",
@@ -332,8 +334,8 @@
         compiler_params=params(),
         name="level2",
     )(parts, level2_inv, level2_basis, fine_index, coarse_index, interior, weight, basis)
+    far = lax.ppermute(far, "wide", [(i, (((i + 1) ^ 1) - 1) % wide) for i in range(wide)])
     near = lax.ppermute(near, "wide", [(i, i ^ 1) for i in range(wide)])
-    far = lax.ppermute(far, "wide", [(i, ((i + 1) ^ 1) - 1) for i in range(1, wide - 1)])
     packets = lax.all_to_all(send, "wide", 0, 0)
 
     send, hot, owner = pl.pallas_call(

time: 53.4 us -> 51.7 us (0.968)
  waiting for transfers between devices: 0.32 us -> 2.75 us
  Pallas kernels: 12.8 us -> 10.4 us
  starting transfers between devices: 14.2 us -> 12.4 us
    pallas_call x1, Pallas kernels: 6.5 us -> 4.08 us  [per_device(): pl.pallas_call(functools.partial(interior_kernel, spans=spans), out_shape...]
    all_to_all x1, waiting for transfers between devices: 0.32 us -> 2.74 us  [per_device(): parts = lax.all_to_all(send, 'narrow', 0, 0)]
    ppermute x1, starting transfers between devices: 3.02 us -> 1.2 us  [per_device(): lax.ppermute(far, 'wide', [(i, ((i + 1 ^ 1) - 1) % wide) for i in range(w...]
  transfers between devices with their start and end apart: 3 -> 3, of which waited for: 1 -> 1; matrix products, arithmetic and copies ran while one was open for 0% -> 0% of each run, Pallas kernels for 14% -> 9%
where the time goes in v3:
time: 51.7 us; the launch traced here: 51.4 us
  blocking collectives  25.8 us (50%)
  starting transfers between devices  12.4 us (24%)
  Pallas kernels  10.4 us (20%)
  waiting for transfers between devices  2.75 us (5%)
    all_to_all x1, blocking collectives, per_device(): packets = lax.all_to_all(send, 'wide', 0, 0)  14.5 us
    all_to_all x1, blocking collectives, per_device(): corr = lax.all_to_all(send, 'wide', 0, 0)  11.3 us
    all_to_all x1, starting transfers between devices, per_device(): parts = lax.all_to_all(send, 'narrow', 0, 0)  9.03 us
    pallas_call x1, Pallas kernels, per_device(): pl.pallas_call(functools.partial(interior_kernel, spans=spans), out_shape...  4.08 us
    pallas_call x1, Pallas kernels, per_device(): pl.pallas_call(head_kernel, out_shape=(jax.ShapeDtypeStruct(fine_basis.sh...  2.87 us
    all_to_all x1, waiting for transfers between devices, per_device(): parts = lax.all_to_all(send, 'narrow', 0, 0)  2.74 us
    ppermute x1, starting transfers between devices, per_device(): near = lax.ppermute(near, 'wide', [(i, i ^ 1) for i in range(wide)])  2.19 us
    pallas_call x1, Pallas kernels, per_device(): pl.pallas_call(tail_kernel, out_shape=jax.ShapeDtypeStruct((loads, width)...  2.11 us
  transfers between devices with their start and end apart: 3, of which 1 were waited for; matrix products, arithmetic and copies ran while one was open for 0% of the time, Pallas kernels for 9%

profile of v3, /device:TPU:1, one launch (start us, length us, event | category | flops | bytes accessed | tf_op | source)
XLA Modules:
  0.0 51.4 jit_solution(16829728683929836214)
XLA Ops:
  0.0 2.9 %head.1 = (bf16[9216,128]{1,0:T(8,128)(2,1)S(1)}, bf16[4,9216]{1,0:T(4,128)(2,1)S(1)}, f32[1,9216]{1,0:T(1,128)S(1)}, f32[1,9216]{1,0:T(1,128)S(1)}, bf16[8,16,128]{2,1,0:T(8,128)(2,1)}) custom-call(f32[4,9216]{1,0:T(4,128)} %resid_hbm.1, s32[1,9216]{1,0:T(1,128)} %bitcast.1, bf16[9216,128]{1,0:T(8,128)(2,1)} %basis_hbm.1, s32[1,128]{1,0:T(1,128)} %index_ref.1), custom_call_target="tpu_custom_call" | custom-call | tf_op jit(solution)/shard_map/head/pallas_call | solution.py:287
  2.9 9.0 %all-to-all-start = ((bf16[8,16,128]{2,1,0:T(8,128)(2,1)}), bf16[8,16,128]{2,1,0:T(8,128)(2,1)S(1)}, u32[]{:S(2)}, u32[]{:S(2)}) async-start(bf16[8,16,128]{2,1,0:T(8,128)(2,1)} %get-tuple-element.18), calls=%async_computation | async-start | bytes 65536 | tf_op jit(solution)/shard_map/all_to_all | solution.py:307
  11.9 0.0 copy-start
  11.9 0.0 copy-start.2
  11.9 0.0 copy-start.3
  11.9 0.0 copy-start.4
  11.9 4.1 %interior.1.interior_ref = f32[4,9216]{1,0:T(4,128)S(1)} custom-call(bf16[4,9216]{1,0:T(4,128)(2,1)S(1)} %get-tuple-element.19.weighted_ref, bf16[24,384,384]{2,1,0:T(8,128)(2,1)} %blocks_hbm.1), custom_call_target="tpu_custom_call" | custom-call | flops 113246208 | bytes 7077888 | tf_op jit(solution)/shard_map/interior/pallas_call | solution.py:310
  16.0 0.0 copy-start.1
  16.0 2.7 %all-to-all-done.parts_ref = bf16[8,16,128]{2,1,0:T(8,128)(2,1)S(1)} async-done(((bf16[8,16,128]{2,1,0:T(8,128)(2,1)}), bf16[8,16,128]{2,1,0:T(8,128)(2,1)S(1)}, u32[]{:S(2)}, u32[]{:S(2)}) %all-to-all-start) | async-done | bytes 32800 | tf_op jit(solution)/shard_map/all_to_all | solution.py:307
  18.8 0.0 copy-done
  18.8 0.0 copy-done.2
  18.8 0.0 copy-done.3
  18.8 0.0 copy-done.4
  18.8 0.6 %level2.1 = (f32[16,128]{1,0:T(8,128)S(1)}, bf16[32,16,128]{2,1,0:T(8,128)(2,1)S(1)}, bf16[128,128]{1,0:T(8,128)(2,1)S(1)}, bf16[1328,128]{1,0:T(8,128)(2,1)S(1)}, bf16[1328,128]{1,0:T(8,128)(2,1)S(1)}) custom-call(bf16[8,16,128]{2,1,0:T(8,128)(2,1)S(1)} %all-to-all-done.parts_ref, bf16[512,512]{1,0:T(8,128)(2,1)S(1)} %copy-done, ...), custom_call_target="tpu_custom_call" | custom-call | tf_op jit(solution)/shard_map/level2/pallas_call | solution.py:322
  19.4 2.2 %collective-permute-start = (bf16[1328,128]{1,0:T(8,128)(2,1)S(1)}, bf16[1328,128]{1,0:T(8,128)(2,1)S(1)}, u32[]{:S(2)}, u32[]{:S(2)}) collective-permute-start(bf16[1328,128]{1,0:T(8,128)(2,1)S(1)} %get-tuple-element.28), channel_id=1, source_target_pairs={{0,8},{8,0},{16,24},{24,16},{32,40},{40,32},{48,56},{56,48},{64,72... | collective-permute-start | bytes 1019912 | tf_op jit(solution)/shard_map/ppermute | solution.py:338
  21.6 1.2 %collective-permute-start.1 = (bf16[1328,128]{1,0:T(8,128)(2,1)S(1)}, bf16[1328,128]{1,0:T(8,128)(2,1)S(1)}, u32[]{:S(2)}, u32[]{:S(2)}) collective-permute-start(bf16[1328,128]{1,0:T(8,128)(2,1)S(1)} %get-tuple-element.29), channel_id=1, source_target_pairs={{0,248},{8,16},{16,8},{24,32},{32,24},{40,48},{48,40},{56,64},{64,... | collective-permute-start | bytes 1019912 | tf_op jit(solution)/shard_map/ppermute | solution.py:337
  22.8 14.5 %all_to_all.15.packets_ref = bf16[32,16,128]{2,1,0:T(8,128)(2,1)S(1)} all-to-all(bf16[32,16,128]{2,1,0:T(8,128)(2,1)S(1)} %get-tuple-element.22), channel_id=1, replica_groups=mesh['wide'=32,'narrow'=8] {'wide'}, dimensions={0} | all-to-all | bytes 262144 | tf_op jit(solution)/shard_map/all_to_all | solution.py:339
  37.3 0.0 copy-done.1
  37.3 0.7 %coarse.1 = (bf16[32,16,128]{2,1,0:T(8,128)(2,1)S(1)}, bf16[128,384]{1,0:T(8,128)(2,1)S(1)}, s32[8,384]{1,0:T(8,128)S(1)}) custom-call(bf16[32,16,128]{2,1,0:T(8,128)(2,1)S(1)} %all_to_all.15.packets_ref, bf16[64,2048]{1,0:T(8,128)(2,1)S(1)} %copy-done.1, s32[1,128]{1,0:T(1,128)S(1)} %copy-done.3), custom_call_target="tpu_custom_call" | custom-call | tf_op jit(solution)/shard_map/coarse/pallas_call | solution.py:341
  38.0 11.3 %all_to_all.16.corr_ref = bf16[32,16,128]{2,1,0:T(8,128)(2,1)S(1)} all-to-all(bf16[32,16,128]{2,1,0:T(8,128)(2,1)S(1)} %get-tuple-element.23), channel_id=1, replica_groups=mesh['wide'=32,'narrow'=8] {'wide'}, dimensions={0} | all-to-all | bytes 262144 | tf_op jit(solution)/shard_map/all_to_all | solution.py:353
  49.3 0.0 collective-permute-done.near_ref
  49.3 0.0 collective-permute-done.1.far_ref
  49.3 2.1 %tail.1 = f32[4,9216]{1,0:T(4,128)} custom-call(bf16[32,16,128]{2,1,0:T(8,128)(2,1)S(1)} %all_to_all.16.corr_ref, bf16[32,16,128]{2,1,0:T(8,128)(2,1)S(1)} %all_to_all.15.packets_ref, bf16[128,384]{1,0:T(8,128)(2,1)S(1)} %get-tuple-element.24.hot_ref, s32[8,384]{1,0:T(8,128)S(1)} %get-tuple-element.25.owner_ref, f32[16,128]{1,0:T(8,128)S(1)} %get-tuple-element.26.local_ref, ...), custom_call_target="tpu_custom_call" | custom-call | tf_op jit(solution)/shard_map/tail/pallas_call | solution.py:355
Async XLA Ops:
  2.9 15.9 %all-to-all-start = ((bf16[8,16,128]{2,1,0:T(8,128)(2,1)}), bf16[8,16,128]{2,1,0:T(8,128)(2,1)S(1)}, u32[]{:S(2)}, u32[]{:S(2)}) async-start(bf16[8,16,128]{2,1,0:T(8,128)(2,1)} %get-tuple-element.18), calls=%async_computation | async-start | bytes 65536 | tf_op jit(solution)/shard_map/all_to_all | solution.py:307
  11.9 6.9 %copy-start = (bf16[512,512]{1,0:T(8,128)(2,1)S(1)}, bf16[512,512]{1,0:T(8,128)(2,1)}, u32[]{:S(2)}) copy-start(bf16[512,512]{1,0:T(8,128)(2,1)} %inverse_ref.2) | copy-start | bytes 1572868
  11.9 6.9 %copy-start.2 = (bf16[512,128]{1,0:T(8,128)(2,1)S(1)}, bf16[512,128]{1,0:T(8,128)(2,1)}, u32[]{:S(2)}) copy-start(bf16[512,128]{1,0:T(8,128)(2,1)} %level2_basis_ref.1) | copy-start | bytes 393220
  11.9 6.9 %copy-start.3 = (s32[1,128]{1,0:T(1,128)S(1)}, s32[1,128]{1,0:T(1,128)}, u32[]{:S(2)}) copy-start(s32[1,128]{1,0:T(1,128)} %coarse_index_ref.3) | copy-start | bytes 1540
  11.9 6.9 %copy-start.4 = (s32[1,128]{1,0:T(1,128)S(1)}, s32[1,128]{1,0:T(1,128)}, u32[]{:S(2)}) copy-start(s32[1,128]{1,0:T(1,128)} %index_ref.1) | copy-start | bytes 1540
  16.0 21.2 %copy-start.1 = (bf16[64,2048]{1,0:T(8,128)(2,1)S(1)}, bf16[64,2048]{1,0:T(8,128)(2,1)}, u32[]{:S(2)}) copy-start(bf16[64,2048]{1,0:T(8,128)(2,1)} %inverse_ref.3) | copy-start | bytes 786436
  19.4 29.9 %collective-permute-start = (bf16[1328,128]{1,0:T(8,128)(2,1)S(1)}, bf16[1328,128]{1,0:T(8,128)(2,1)S(1)}, u32[]{:S(2)}, u32[]{:S(2)}) collective-permute-start(bf16[1328,128]{1,0:T(8,128)(2,1)S(1)} %get-tuple-element.28), channel_id=1, source_target_pairs={{0,8},{8,0},{16,24},{24,16},{32,40},{40,32},{48,56},{56,48},{64,72... | collective-permute-start | bytes 1019912 | tf_op jit(solution)/shard_map/ppermute | solution.py:338
  21.6 27.7 %collective-permute-start.1 = (bf16[1328,128]{1,0:T(8,128)(2,1)S(1)}, bf16[1328,128]{1,0:T(8,128)(2,1)S(1)}, u32[]{:S(2)}, u32[]{:S(2)}) collective-permute-start(bf16[1328,128]{1,0:T(8,128)(2,1)S(1)} %get-tuple-element.29), channel_id=1, source_target_pairs={{0,248},{8,16},{16,8},{24,32},{32,24},{40,48},{48,40},{56,64},{64,... | collective-permute-start | bytes 1019912 | tf_op jit(solution)/shard_map/ppermute | solution.py:337

commit v4 on v3

v4 whole, which is shorter than its diff:
```python
import functools

import jax
import jax.numpy as jnp
from jax import lax
from jax.experimental import pallas as pl
from jax.experimental.pallas import tpu as pltpu
from jax.sharding import PartitionSpec as P

NF = 1152
LANES = 128
REST = 64
LOCAL = 48
F32 = jnp.float32
BF16 = jnp.bfloat16
LIMIT = 16 * 1024 * 1024
NN = (((1,), (0,)), ((), ()))
NT = (((1,), (1,)), ((), ()))
VMEM = pl.BlockSpec(memory_space=pltpu.VMEM)


def mm(a, b, dims=NN):
    return lax.dot_general(a, b, dims, preferred_element_type=F32)


def split_mm(a, b, dims=NN):
    high = a.astype(BF16)
    rest = a - high.astype(F32)
    mid = rest.astype(BF16)
    low = (rest - mid.astype(F32)).astype(BF16)
    return mm(high, b, dims) + (mm(mid, b, dims) + mm(low, b, dims))


def side_by_side(a, b):
    zero = jnp.zeros_like(a)
    return jnp.concatenate([jnp.concatenate([a, zero], axis=1), jnp.concatenate([zero, b], axis=1)], axis=0).astype(BF16)


def selector(index_row, width):
    column = jnp.transpose(jnp.broadcast_to(index_row.astype(F32), (LANES, LANES)))
    lane = lax.broadcasted_iota(jnp.int32, (LANES, LANES), 1).astype(F32)
    return jnp.concatenate(
        [jnp.where(column == lane + float(q * LANES), 1.0, 0.0) for q in range(width // LANES)], axis=1
    ).astype(BF16)


def sides(width):
    me, count = lax.axis_index("wide"), lax.axis_size("wide")
    odd = lax.rem(me, 2)
    last = width - NF
    far = me - 1 + 2 * odd
    inside = jnp.logical_and(far >= 0, far < count)
    return (
        (pl.multiple_of(last * (1 - odd), LANES), me + 1 - 2 * odd, None),
        (pl.multiple_of(last * odd, LANES), jnp.clip(far, 0, count - 1), inside),
    )


def copies_of(pairs, sems):
    copies = [pltpu.make_async_copy(source, target, sems.at[at]) for at, (source, target) in enumerate(pairs)]
    for copy in copies:
        copy.start()
    return copies


def head_kernel(
    resid_hbm,
    mult_hbm,
    basis_hbm,
    index_hbm,
    basis_ref,
    weighted_ref,
    inverse_ref,
    send_ref,
    resid_ref,
    mult_ref,
    index_ref,
    sems,
):
    width = resid_ref.shape[1]
    level_width = 4 * LANES
    loads = resid_ref.shape[0]
    parts = sems.shape[0] - 3
    step = width // parts
    cuts = [slice(part * step, (part + 1) * step) for part in range(parts)]
    copies = copies_of(
        [(mult_hbm, mult_ref), (resid_hbm, resid_ref), (index_hbm, index_ref)]
        + [(basis_hbm.at[cut], basis_ref.at[cut]) for cut in cuts],
        sems,
    )
    copies[0].wait()
    inverse = 1.0 / mult_ref[...].astype(F32)
    inverse_ref[...] = inverse
    copies[1].wait()
    weighted = resid_ref[...] * inverse
    weighted_ref[...] = weighted.astype(BF16)
    copies[2].wait()
    select = selector(index_ref[...], level_width)
    total = jnp.zeros((2 * loads, 2 * LANES), F32)
    for part, cut in enumerate(cuts):
        copies[3 + part].wait()
        first, second = slice(cut.start, cut.start + step // 2), slice(cut.start + step // 2, cut.stop)
        total += mm(
            jnp.concatenate([weighted[:, first], weighted[:, second]], axis=0).astype(BF16),
            jnp.concatenate([basis_ref[first, :], basis_ref[second, :]], axis=1),
        )
    total = total[:loads, :LANES] + total[loads:, LANES:]
    contrib = split_mm(total, select)
    chunk = jnp.concatenate(
        [contrib[:, q * LANES : (q + 1) * LANES] for q in range(level_width // LANES)], axis=0
    ).astype(BF16)
    for other in range(send_ref.shape[0]):
        send_ref[other] = chunk


def interior_kernel(weighted_ref, blocks_hbm, coarse_inv_hbm, interior_ref, tiles_ref, blocks_ref, sems, *, spans):
    size = blocks_ref.shape[1]
    whole = size // 256 * 256
    cuts = [pl.ds(first, blocks) for first, blocks in spans]
    pairs = [(blocks_hbm.at[cut], blocks_ref.at[cut]) for cut in cuts]
    pairs += [(coarse_inv_hbm.at[:, pl.ds(h * LANES, LANES)], tiles_ref.at[h]) for h in range(tiles_ref.shape[0])]
    copies = copies_of(pairs, sems)
    for copy, (first, blocks) in zip(copies, spans):
        copy.wait()
        for b in range(first, first + blocks, 2):
            one, two = slice(b * size, (b + 1) * size), slice((b + 1) * size, (b + 2) * size)
            left, right = weighted_ref[:, one].astype(F32), weighted_ref[:, two].astype(F32)
            rest = mm(
                side_by_side(left[:, whole:], right[:, whole:]),
                jnp.concatenate([blocks_ref[b][:, whole:], blocks_ref[b + 1][:, whole:]], axis=1),
                NT,
            )
            loads = left.shape[0]
            first_sum = mm(left[:, :whole].astype(BF16), blocks_ref[b][:, :whole], NT) + rest[:loads]
            second_sum = mm(right[:, :whole].astype(BF16), blocks_ref[b + 1][:, :whole], NT) + rest[loads:]
            interior_ref[:, one] = first_sum.astype(BF16)
            interior_ref[:, two] = second_sum.astype(BF16)
    for copy in copies[len(spans) :]:
        copy.wait()


def level2_kernel(
    parts_ref,
    inverse_ref,
    level2_basis_ref,
    index_ref,
    coarse_index_ref,
    interior_ref,
    inverse_mult_ref,
    basis_ref,
    tiles_ref,
    local_ref,
    send_ref,
    picked_ref,
    near_ref,
    far_ref,
    packet,
    stage,
):
    loads, width = interior_ref.shape
    rows = stage.shape[0]
    total = jnp.sum(parts_ref[...].astype(F32), axis=0)
    low = jnp.concatenate([total[q * loads : (q + 1) * loads] for q in range(total.shape[0] // loads)], axis=1).astype(BF16)
    local = mm(low, inverse_ref[...], NT)
    select = selector(index_ref[...], level2_basis_ref.shape[0])
    chosen = mm(select, level2_basis_ref[...]).astype(BF16)
    picked_ref[...] = chosen
    local_picked = split_mm(local, select, NT)
    local_ref[...] = local_picked
    coarse = coarse_index_ref[...]
    packet[:loads, :] = mm(low, level2_basis_ref[...])
    packet[loads : loads + 1, :] = (coarse // LANES).astype(F32)
    packet[loads + 1 : loads + 2, :] = (coarse % LANES).astype(F32)
    packet[loads + 2 :, :] = jnp.zeros((packet.shape[0] - loads - 2, LANES), F32)
    chunk = packet[...].astype(BF16)
    for other in range(send_ref.shape[0]):
        send_ref[other] = chunk

    pieces = NF // LANES
    for out_ref, (start, _, _) in zip((near_ref, far_ref), sides(width)):
        out_ref[:NF, :] = basis_ref[pl.ds(start, NF), :]
        out_ref[NF : NF + LANES, :] = chosen
        stage[loads * pieces :, :] = jnp.zeros((rows - loads * pieces, LANES), F32)
        for q in range(pieces):
            lanes = pl.ds(pl.multiple_of(start + q * LANES, LANES), LANES)
            stage[q * loads : (q + 1) * loads, :] = interior_ref[:, lanes].astype(F32)
            stage[loads * pieces + q : loads * pieces + q + 1, :] = jnp.round(1.0 / inverse_mult_ref[:, lanes])
        stage[LOCAL : LOCAL + loads, :] = local_picked
        out_ref[NF + LANES : NF + LANES + rows, :] = stage[...].astype(BF16)
    count = tiles_ref.shape[1]
    for h in range(tiles_ref.shape[0]):
        at = NF + LANES + rows + h * count
        near_ref[at : at + count, :] = tiles_ref[h]


def coarse_kernel(packets_ref, tiles_ref, coarse_index_ref, near_ref, send_ref, hot_ref, owner_ref, *, width):
    loads = 4
    groups, rows = packets_ref.shape[0], packets_ref.shape[1]
    highs, count = tiles_ref.shape[0], tiles_ref.shape[1]
    row = lax.broadcasted_iota(jnp.int32, (LANES, LANES), 0).astype(F32)
    tall, hot = [], []
    for g in range(groups):
        packet = packets_ref[g].astype(F32)
        high = jnp.broadcast_to(packet[loads : loads + 1], (rows, LANES))
        low = jnp.broadcast_to(packet[loads + 1 : loads + 2], (LANES, LANES))
        tall.append(jnp.concatenate([jnp.where(high == float(h), packet, 0.0) for h in range(highs)], axis=0).astype(BF16))
        hot.append(jnp.where(row == low, 1.0, 0.0).astype(BF16))
    total = mm(jnp.concatenate(tall, axis=1), jnp.concatenate(hot, axis=1), NT)
    coarse_low = jnp.concatenate([total[rows * h : rows * (h + 1)] for h in range(highs)], axis=1).astype(BF16)
    own = mm(coarse_low, jnp.concatenate([tiles_ref[h] for h in range(highs)], axis=1), NT)
    first = near_ref.shape[0] - highs * count
    theirs = jnp.concatenate([near_ref[first + h * count : first + (h + 1) * count, :] for h in range(highs)], axis=1)
    other = mm(coarse_low, theirs, NT)
    odd = lax.rem(lax.axis_index("wide"), 2) == 1
    chunk = jnp.concatenate([jnp.where(odd, other, own), jnp.where(odd, own, other)], axis=1).astype(BF16)
    for at in range(send_ref.shape[0]):
        send_ref[at] = chunk

    packets = [packets_ref[group].astype(F32) for _, group, _ in sides(width)]
    coarse = coarse_index_ref[...]
    owner = jnp.concatenate([(coarse // LANES).astype(F32)] + [p[loads : loads + 1] for p in packets], axis=1)
    within = jnp.concatenate([(coarse % LANES).astype(F32)] + [p[loads + 1 : loads + 2] for p in packets], axis=1)
    shape = (LANES, within.shape[1])
    lane = lax.broadcasted_iota(jnp.int32, shape, 0).astype(F32)
    hot_ref[...] = jnp.where(lane == jnp.broadcast_to(within, shape), 1.0, 0.0).astype(BF16)
    owner_ref[...] = jnp.broadcast_to(owner, owner_ref.shape)


def tail_kernel(
    corr_ref,
    hot_ref,
    owner_ref,
    local_ref,
    picked_ref,
    near_ref,
    far_ref,
    interior_ref,
    inverse_ref,
    basis_ref,
    out_hbm,
    out_ref,
    sems,
):
    loads, width = interior_ref.shape
    half = width // 2
    pieces = NF // LANES
    chips, rows = corr_ref.shape[0], corr_ref.shape[1]
    table = jnp.concatenate([corr_ref[c].astype(F32) for c in range(chips)], axis=0).astype(BF16)
    picks = mm(table, hot_ref[...])
    owner = owner_ref[...]
    picked = jnp.zeros(owner.shape, F32)
    for c in range(chips):
        picked += jnp.where(owner == float(c), picks[rows * c : rows * (c + 1)], 0.0)
    picked = picked.astype(BF16)
    gathered = local_ref[...] + mm(picked[:, :LANES], picked_ref[...], NT)[:loads]
    gathered = side_by_side(gathered, gathered)
    theirs, rests = [], []
    for side, face_ref in enumerate((near_ref, far_ref)):
        lanes = slice((side + 1) * LANES, (side + 2) * LANES)
        rest = face_ref[NF + LANES : NF + LANES + REST, :].astype(F32)
        theirs.append(rest[LOCAL : LOCAL + loads] + mm(picked[:, lanes], face_ref[NF : NF + LANES, :], NT)[:loads])
        rests.append(rest)
    shifts = mm(side_by_side(*theirs), jnp.concatenate([near_ref[:NF, :], far_ref[:NF, :]], axis=1), NT)

    copies = []

    def piece(at, count):
        one, two = slice(at, at + count), slice(half + at, half + at + count)
        shift = mm(gathered, jnp.concatenate([basis_ref[one, :], basis_ref[two, :]], axis=1), NT)
        out_ref[:, one] = (interior_ref[:, one].astype(F32) + shift[:loads]) * inverse_ref[:, one]
        out_ref[:, two] = (interior_ref[:, two].astype(F32) + shift[loads:]) * inverse_ref[:, two]
        return one, two

    def send(cut):
        copy = pltpu.make_async_copy(out_ref.at[:, cut], out_hbm.at[:, cut], sems.at[len(copies)])
        copy.start()
        copies.append(copy)

    cuts = piece(0, half // 2) + piece(half // 2, half // 2)
    send(cuts[1])
    send(cuts[2])
    for side, (start, _, exists) in enumerate(sides(width)):
        rest, shift = rests[side], shifts[side * loads : (side + 1) * loads]
        scale = 1.0 / rest[loads * pieces : loads * pieces + pieces]
        if exists is not None:
            scale = jnp.where(exists, scale, 0.0)
        for q in range(pieces):
            face = (rest[q * loads : (q + 1) * loads] + shift[:, q * LANES : (q + 1) * LANES]) * scale[q : q + 1]
            at = pl.ds(pl.multiple_of(start + q * LANES, LANES), LANES)
            out_ref[:, at] = out_ref[:, at] + face
    send(cuts[0])
    send(cuts[3])
    for copy in copies:
        copy.wait()


def params(limit=LIMIT):
    return pltpu.CompilerParams(vmem_limit_bytes=limit)


def per_device(
    resid,
    mult,
    dirichlet_inv,
    fine_basis,
    fine_index,
    level2_inv,
    level2_basis,
    coarse_index,
    coarse_inv,
):
    loads, width = resid.shape
    blocks, size = dirichlet_inv.shape[0], dirichlet_inv.shape[1]
    wide, narrow = lax.axis_size("wide"), lax.axis_size("narrow")
    mult = mult.reshape(1, width)

    pieces = 4
    hbm = pl.BlockSpec(memory_space=pltpu.HBM)

    def pinned(*arrays):
        return [pltpu.with_memory_space_constraint(array, pltpu.HBM) for array in arrays]

    basis, weighted, inverse, send = pl.pallas_call(
        head_kernel,
        out_shape=(
            jax.ShapeDtypeStruct(fine_basis.shape, BF16),
            jax.ShapeDtypeStruct((loads, width), BF16),
            jax.ShapeDtypeStruct((1, width), F32),
            jax.ShapeDtypeStruct((narrow, 16, LANES), BF16),
        ),
        in_specs=[hbm] * 4,
        out_specs=(VMEM,) * 4,
        scratch_shapes=[
            pltpu.VMEM(resid.shape, F32),
            pltpu.VMEM(mult.shape, jnp.int32),
            pltpu.VMEM(fine_index.shape, jnp.int32),
            pltpu.SemaphoreType.DMA((3 + pieces,)),
        ],
        compiler_params=params(),
        name="head",
    )(*pinned(resid, mult, fine_basis, fine_index))
    parts = lax.all_to_all(send, "narrow", 0, 0)
    sixth = blocks // 6
    spans = tuple((at, sixth) for at in range(0, blocks, sixth))
    highs = coarse_inv.shape[1] // LANES
    interior, tiles = pl.pallas_call(
        functools.partial(interior_kernel, spans=spans),
        out_shape=(
            jax.ShapeDtypeStruct((loads, width), BF16),
            jax.ShapeDtypeStruct((highs, coarse_inv.shape[0], LANES), BF16),
        ),
        input_output_aliases={0: 0},
        in_specs=[VMEM, hbm, hbm],
        out_specs=(VMEM, VMEM),
        scratch_shapes=[pltpu.VMEM(dirichlet_inv.shape, BF16), pltpu.SemaphoreType.DMA((len(spans) + highs,))],
        compiler_params=params(),
        cost_estimate=pl.CostEstimate(flops=2 * 16 * blocks * size * size, bytes_accessed=2 * blocks * size * size, transcendentals=0),
        name="interior",
    )(weighted, *pinned(dirichlet_inv, coarse_inv))

    near_rows = NF + LANES + REST + coarse_inv.size // LANES
    local, send, chosen, near, far = pl.pallas_call(
        level2_kernel,
        out_shape=(
            jax.ShapeDtypeStruct((loads, LANES), F32),
            jax.ShapeDtypeStruct((wide, 8, LANES), BF16),
            jax.ShapeDtypeStruct((LANES, LANES), BF16),
            jax.ShapeDtypeStruct((near_rows, LANES), BF16),
            jax.ShapeDtypeStruct((NF + LANES + REST, LANES), BF16),
        ),
        in_specs=[VMEM] * 9,
        out_specs=(VMEM,) * 5,
        scratch_shapes=[
            pltpu.VMEM((8, LANES), F32),
            pltpu.VMEM((REST, LANES), F32),
        ],
        compiler_params=params(),
        name="level2",
    )(parts, level2_inv, level2_basis, fine_index, coarse_index, interior, inverse, basis, tiles)
    far = lax.ppermute(far, "wide", [(i, (((i + 1) ^ 1) - 1) % wide) for i in range(wide)])
    near = lax.ppermute(near, "wide", [(i, i ^ 1) for i in range(wide)])
    packets = lax.all_to_all(send, "wide", 0, 0)

    send, hot, owner = pl.pallas_call(
        functools.partial(coarse_kernel, width=width),
        out_shape=(
            jax.ShapeDtypeStruct((wide // 2, 8, LANES), BF16),
            jax.ShapeDtypeStruct((LANES, 3 * LANES), BF16),
            jax.ShapeDtypeStruct((8, 3 * LANES), F32),
        ),
        in_specs=[VMEM] * 4,
        out_specs=(VMEM,) * 3,
        compiler_params=params(),
        name="coarse",
    )(packets, tiles, coarse_index, near)
    send, near, far = lax.optimization_barrier((send, near, far))
    cores = [[chip * 2 + core for chip in range(wide // 2)] for core in range(2)]
    corr = lax.all_to_all(send, "wide", 0, 0, axis_index_groups=cores)

    return pl.pallas_call(
        tail_kernel,
        out_shape=jax.ShapeDtypeStruct((loads, width), F32),
        in_specs=[VMEM] * 10,
        out_specs=hbm,
        scratch_shapes=[pltpu.VMEM((loads, width), F32), pltpu.SemaphoreType.DMA((4,))],
        compiler_params=params(),
        name="tail",
    )(corr, hot, owner, local, chosen, near, far, interior, inverse, basis)


def solution(mesh):
    placed = (
        P(None, ("wide", "narrow")),
        P(("wide", "narrow")),
        P(("wide", "narrow"), None, None),
        P(("wide", "narrow"), None),
        P(("wide", "narrow"), None),
        P("wide", None),
        P("wide", None),
        P("wide", None),
        P("wide", None),
    )
    return jax.shard_map(
        per_device,
        mesh=mesh,
        in_specs=placed,
        out_specs=P(None, ("wide", "narrow")),
        check_vma=False,
    )
```

time: 51.7 us -> 49.1 us (0.950)
  blocking collectives: 25.8 us -> 23.3 us
    all_to_all x1, blocking collectives: 11.3 us -> 9.14 us  [per_device(): corr = lax.all_to_all(send, 'wide', 0, 0, axis_index_groups=cores)]
  transfers between devices with their start and end apart: 3 -> 3, of which waited for: 1 -> 1; matrix products, arithmetic and copies ran while one was open for 0% -> 0% of each run, Pallas kernels for 9% -> 10%
where the time goes in v4:
time: 49.1 us; the launch traced here: 48.9 us
  blocking collectives  23.3 us (47%)
  starting transfers between devices  12.4 us (25%)
  Pallas kernels  10.4 us (21%)
  waiting for transfers between devices  2.72 us (6%)
    all_to_all x1, blocking collectives, per_device(): packets = lax.all_to_all(send, 'wide', 0, 0)  14.2 us
    all_to_all x1, blocking collectives, per_device(): corr = lax.all_to_all(send, 'wide', 0, 0, axis_index_groups=cores)  9.14 us
    all_to_all x1, starting transfers between devices, per_device(): parts = lax.all_to_all(send, 'narrow', 0, 0)  9.03 us
    pallas_call x1, Pallas kernels, per_device(): pl.pallas_call(functools.partial(interior_kernel, spans=spans), out_shape...  4.12 us
    pallas_call x1, Pallas kernels, per_device(): pl.pallas_call(head_kernel, out_shape=(jax.ShapeDtypeStruct(fine_basis.sh...  2.87 us
    all_to_all x1, waiting for transfers between devices, per_device(): parts = lax.all_to_all(send, 'narrow', 0, 0)  2.71 us
    ppermute x1, starting transfers between devices, per_device(): near = lax.ppermute(near, 'wide', [(i, i ^ 1) for i in range(wide)])  2.18 us
    pallas_call x1, Pallas kernels, per_device(): pl.pallas_call(tail_kernel, out_shape=jax.ShapeDtypeStruct((loads, width)...  1.85 us
  transfers between devices with their start and end apart: 3, of which 1 were waited for; matrix products, arithmetic and copies ran while one was open for 0% of the time, Pallas kernels for 10%

profile of v4, /device:TPU:1, one launch (start us, length us, event | category | flops | bytes accessed | tf_op | source)
XLA Modules:
  0.0 48.9 jit_solution(1591051204950278769)
XLA Ops:
  0.0 2.9 %head.1 = (bf16[9216,128]{1,0:T(8,128)(2,1)S(1)}, bf16[4,9216]{1,0:T(4,128)(2,1)S(1)}, f32[1,9216]{1,0:T(1,128)S(1)}, bf16[8,16,128]{2,1,0:T(8,128)(2,1)}) custom-call(f32[4,9216]{1,0:T(4,128)} %resid_hbm.1, s32[1,9216]{1,0:T(1,128)} %bitcast.1, bf16[9216,128]{1,0:T(8,128)(2,1)} %basis_hbm.1, s32[1,128]{1,0:T(1,128)} %index_ref.1), custom_call_target="tpu_custom_call" | custom-call | tf_op jit(solution)/shard_map/head/pallas_call | solution.py:323
  2.9 9.0 %all-to-all-start = ((bf16[8,16,128]{2,1,0:T(8,128)(2,1)}), bf16[8,16,128]{2,1,0:T(8,128)(2,1)S(1)}, u32[]{:S(2)}, u32[]{:S(2)}) async-start(bf16[8,16,128]{2,1,0:T(8,128)(2,1)} %get-tuple-element.22), calls=%async_computation | async-start | bytes 65536 | tf_op jit(solution)/shard_map/all_to_all | solution.py:342
  11.9 0.0 copy-start
  11.9 0.0 copy-start.1
  11.9 0.0 copy-start.2
  11.9 0.0 copy-start.3
  11.9 4.1 %interior.1 = (bf16[4,9216]{1,0:T(4,128)(2,1)S(1)}, bf16[16,64,128]{2,1,0:T(8,128)(2,1)S(1)}) custom-call(bf16[4,9216]{1,0:T(4,128)(2,1)S(1)} %get-tuple-element.23.weighted_ref, bf16[24,384,384]{2,1,0:T(8,128)(2,1)} %blocks_hbm.1, bf16[64,2048]{1,0:T(8,128)(2,1)} %coarse_inv_hbm.1), custom_call_target="tpu_custom_call", output_to_operand_aliasing={{0}: (0, {})} | custom-call | flops 113246208 | bytes 7077888 | tf_op jit(solution)/shard_map/interior/pallas_call | solution.py:346
  16.1 2.7 %all-to-all-done.parts_ref = bf16[8,16,128]{2,1,0:T(8,128)(2,1)S(1)} async-done(((bf16[8,16,128]{2,1,0:T(8,128)(2,1)}), bf16[8,16,128]{2,1,0:T(8,128)(2,1)S(1)}, u32[]{:S(2)}, u32[]{:S(2)}) %all-to-all-start) | async-done | bytes 32800 | tf_op jit(solution)/shard_map/all_to_all | solution.py:342
  18.8 0.0 copy-done
  18.8 0.0 copy-done.1
  18.8 0.0 copy-done.2
  18.8 0.0 copy-done.3
  18.8 0.6 %level2.1 = (f32[4,128]{1,0:T(4,128)S(1)}, bf16[32,8,128]{2,1,0:T(8,128)(2,1)S(1)}, bf16[128,128]{1,0:T(8,128)(2,1)S(1)}, bf16[2368,128]{1,0:T(8,128)(2,1)S(1)}, bf16[1344,128]{1,0:T(8,128)(2,1)S(1)}) custom-call(bf16[8,16,128]{2,1,0:T(8,128)(2,1)S(1)} %all-to-all-done.parts_ref, bf16[512,512]{1,0:T(8,128)(2,1)S(1)} %copy-done, ...), custom_call_target="tpu_custom_call" | custom-call | tf_op jit(solution)/shard_map/level2/pallas_call | solution.py:362
  19.4 2.2 %collective-permute-start = (bf16[2368,128]{1,0:T(8,128)(2,1)S(1)}, bf16[2368,128]{1,0:T(8,128)(2,1)S(1)}, u32[]{:S(2)}, u32[]{:S(2)}) collective-permute-start(bf16[2368,128]{1,0:T(8,128)(2,1)S(1)} %get-tuple-element.29), channel_id=1, source_target_pairs={{0,8},{8,0},{16,24},{24,16},{32,40},{40,32},{48,56},{56,48},{64,72... | collective-permute-start | bytes 1818632 | tf_op jit(solution)/shard_map/ppermute | solution.py:381
  21.6 1.2 %collective-permute-start.1 = (bf16[1344,128]{1,0:T(8,128)(2,1)S(1)}, bf16[1344,128]{1,0:T(8,128)(2,1)S(1)}, u32[]{:S(2)}, u32[]{:S(2)}) collective-permute-start(bf16[1344,128]{1,0:T(8,128)(2,1)S(1)} %get-tuple-element.31), channel_id=1, source_target_pairs={{0,248},{8,16},{16,8},{24,32},{32,24},{40,48},{48,40},{56,64},{64,... | collective-permute-start | bytes 1032200 | tf_op jit(solution)/shard_map/ppermute | solution.py:380
  22.8 14.2 %all_to_all.15.packets_ref = bf16[32,8,128]{2,1,0:T(8,128)(2,1)S(1)} all-to-all(bf16[32,8,128]{2,1,0:T(8,128)(2,1)S(1)} %get-tuple-element.28), channel_id=1, replica_groups=mesh['wide'=32,'narrow'=8] {'wide'}, dimensions={0} | all-to-all | bytes 131072 | tf_op jit(solution)/shard_map/all_to_all | solution.py:382
  36.9 0.0 collective-permute-done.near_ref
  36.9 1.0 %coarse.1 = (bf16[16,8,128]{2,1,0:T(8,128)(2,1)S(1)}, bf16[128,384]{1,0:T(8,128)(2,1)S(1)}, f32[8,384]{1,0:T(8,128)S(1)}) custom-call(bf16[32,8,128]{2,1,0:T(8,128)(2,1)S(1)} %all_to_all.15.packets_ref, bf16[16,64,128]{2,1,0:T(8,128)(2,1)S(1)} %get-tuple-element.27.tiles_ref, s32[1,128]{1,0:T(1,128)S(1)} %copy-done.2, ...), custom_call_target="tpu_custom_call" | custom-call | tf_op jit(solution)/shard_map/coarse/pallas_call | solution.py:384
  37.9 0.0 collective-permute-done.1.far_ref
  37.9 9.1 %all_to_all.16.corr_ref = bf16[16,8,128]{2,1,0:T(8,128)(2,1)S(1)} all-to-all(bf16[16,8,128]{2,1,0:T(8,128)(2,1)S(1)} %get-tuple-element.32), channel_id=1, replica_groups={{0,16,32,48,64,80,96,112,128,144,160,176,192,208,224,240},{8,24,40,56,7..., dimensions={0} | all-to-all | bytes 65536 | tf_op jit(solution)/shard_map/all_to_all | solution.py:398
  47.1 1.9 %tail.1 = f32[4,9216]{1,0:T(4,128)} custom-call(bf16[16,8,128]{2,1,0:T(8,128)(2,1)S(1)} %all_to_all.16.corr_ref, bf16[128,384]{1,0:T(8,128)(2,1)S(1)} %get-tuple-element.33.hot_ref, f32[8,384]{1,0:T(8,128)S(1)} %get-tuple-element.34.owner_ref, f32[4,128]{1,0:T(4,128)S(1)} %get-tuple-element.35.local_ref, bf16[128,128]{1,0:T(8,128)(2,1)S(1)} %get-tuple-element.36.picked_ref, ...), custom_call_target="tpu_custom_call" | custom-call | tf_op jit(solution)/shard_map/tail/pallas_call | solution.py:400
Async XLA Ops:
  2.9 15.9 %all-to-all-start = ((bf16[8,16,128]{2,1,0:T(8,128)(2,1)}), bf16[8,16,128]{2,1,0:T(8,128)(2,1)S(1)}, u32[]{:S(2)}, u32[]{:S(2)}) async-start(bf16[8,16,128]{2,1,0:T(8,128)(2,1)} %get-tuple-element.22), calls=%async_computation | async-start | bytes 65536 | tf_op jit(solution)/shard_map/all_to_all | solution.py:342
  11.9 6.9 %copy-start = (bf16[512,512]{1,0:T(8,128)(2,1)S(1)}, bf16[512,512]{1,0:T(8,128)(2,1)}, u32[]{:S(2)}) copy-start(bf16[512,512]{1,0:T(8,128)(2,1)} %inverse_ref.1) | copy-start | bytes 1572868
  11.9 6.9 %copy-start.1 = (bf16[512,128]{1,0:T(8,128)(2,1)S(1)}, bf16[512,128]{1,0:T(8,128)(2,1)}, u32[]{:S(2)}) copy-start(bf16[512,128]{1,0:T(8,128)(2,1)} %level2_basis_ref.1) | copy-start | bytes 393220
  11.9 6.9 %copy-start.2 = (s32[1,128]{1,0:T(1,128)S(1)}, s32[1,128]{1,0:T(1,128)}, u32[]{:S(2)}) copy-start(s32[1,128]{1,0:T(1,128)} %coarse_index_ref.3) | copy-start | bytes 1540
  11.9 6.9 %copy-start.3 = (s32[1,128]{1,0:T(1,128)S(1)}, s32[1,128]{1,0:T(1,128)}, u32[]{:S(2)}) copy-start(s32[1,128]{1,0:T(1,128)} %index_ref.1) | copy-start | bytes 1540
  19.4 17.5 %collective-permute-start = (bf16[2368,128]{1,0:T(8,128)(2,1)S(1)}, bf16[2368,128]{1,0:T(8,128)(2,1)S(1)}, u32[]{:S(2)}, u32[]{:S(2)}) collective-permute-start(bf16[2368,128]{1,0:T(8,128)(2,1)S(1)} %get-tuple-element.29), channel_id=1, source_target_pairs={{0,8},{8,0},{16,24},{24,16},{32,40},{40,32},{48,56},{56,48},{64,72... | collective-permute-start | bytes 1818632 | tf_op jit(solution)/shard_map/ppermute | solution.py:381
  21.6 16.3 %collective-permute-start.1 = (bf16[1344,128]{1,0:T(8,128)(2,1)S(1)}, bf16[1344,128]{1,0:T(8,128)(2,1)S(1)}, u32[]{:S(2)}, u32[]{:S(2)}) collective-permute-start(bf16[1344,128]{1,0:T(8,128)(2,1)S(1)} %get-tuple-element.31), channel_id=1, source_target_pairs={{0,248},{8,16},{16,8},{24,32},{32,24},{40,48},{48,40},{56,64},{64,... | collective-permute-start | bytes 1032200 | tf_op jit(solution)/shard_map/ppermute | solution.py:380

commit v5 on v4

--- a/solution.py
+++ b/solution.py
@@ -113,14 +113,16 @@
         send_ref[other] = chunk
 
 
-def interior_kernel(weighted_ref, blocks_hbm, coarse_inv_hbm, interior_ref, tiles_ref, blocks_ref, sems, *, spans):
+def interior_kernel(weighted_ref, blocks_hbm, coarse_inv_hbm, interior_ref, tiles_ref, blocks_ref, rows_ref, sems, *, spans):
     size = blocks_ref.shape[1]
     whole = size // 256 * 256
     cuts = [pl.ds(first, blocks) for first, blocks in spans]
-    pairs = [(blocks_hbm.at[cut], blocks_ref.at[cut]) for cut in cuts]
-    pairs += [(coarse_inv_hbm.at[:, pl.ds(h * LANES, LANES)], tiles_ref.at[h]) for h in range(tiles_ref.shape[0])]
-    copies = copies_of(pairs, sems)
-    for copy, (first, blocks) in zip(copies, spans):
+    copies = copies_of([(coarse_inv_hbm, rows_ref)] + [(blocks_hbm.at[cut], blocks_ref.at[cut]) for cut in cuts], sems)
+    copies[0].wait()
+    for p in range(tiles_ref.shape[0]):
+        rows = [rows_ref[:, (2 * p + i) * LANES : (2 * p + i + 1) * LANES].astype(F32) for i in range(2)]
+        tiles_ref[p] = jnp.transpose(jnp.concatenate(rows, axis=0)).astype(BF16)
+    for copy, (first, blocks) in zip(copies[1:], spans):
         copy.wait()
         for b in range(first, first + blocks, 2):
             one, two = slice(b * size, (b + 1) * size), slice((b + 1) * size, (b + 2) * size)
@@ -135,8 +137,6 @@
             second_sum = mm(right[:, :whole].astype(BF16), blocks_ref[b + 1][:, :whole], NT) + rest[loads:]
             interior_ref[:, one] = first_sum.astype(BF16)
             interior_ref[:, two] = second_sum.astype(BF16)
-    for copy in copies[len(spans) :]:
-        copy.wait()
 
 
 def level2_kernel(
@@ -196,21 +196,29 @@
 def coarse_kernel(packets_ref, tiles_ref, coarse_index_ref, near_ref, send_ref, hot_ref, owner_ref, *, width):
     loads = 4
     groups, rows = packets_ref.shape[0], packets_ref.shape[1]
-    highs, count = tiles_ref.shape[0], tiles_ref.shape[1]
-    row = lax.broadcasted_iota(jnp.int32, (LANES, LANES), 0).astype(F32)
+    pairs = tiles_ref.shape[0]
+    highs, count = 2 * pairs, tiles_ref.shape[2] // 2
+    row = lax.broadcasted_iota(jnp.int32, (LANES, LANES), 0).astype(F32).astype(BF16)
     tall, hot = [], []
     for g in range(groups):
         packet = packets_ref[g].astype(F32)
-        high = jnp.broadcast_to(packet[loads : loads + 1], (rows, LANES))
-        low = jnp.broadcast_to(packet[loads + 1 : loads + 2], (LANES, LANES))
-        tall.append(jnp.concatenate([jnp.where(high == float(h), packet, 0.0) for h in range(highs)], axis=0).astype(BF16))
-        hot.append(jnp.where(row == low, 1.0, 0.0).astype(BF16))
+        twice = jnp.concatenate([packet, packet], axis=0).astype(BF16)
+        high = jnp.broadcast_to(packet[loads : loads + 1], (2 * rows, LANES))
+        which = jnp.concatenate([jnp.zeros((rows, LANES), F32), jnp.ones((rows, LANES), F32)], axis=0)
+        high = (high - which).astype(BF16)
+        low = jnp.broadcast_to(packet[loads + 1 : loads + 2], (LANES, LANES)).astype(BF16)
+        zero, one = jnp.zeros((), BF16), jnp.ones((), BF16)
+        tall.append(jnp.concatenate([jnp.where(high == jnp.asarray(h, BF16), twice, zero) for h in range(0, highs, 2)], axis=0))
+        hot.append(jnp.where(row == low, one, zero))
     total = mm(jnp.concatenate(tall, axis=1), jnp.concatenate(hot, axis=1), NT)
-    coarse_low = jnp.concatenate([total[rows * h : rows * (h + 1)] for h in range(highs)], axis=1).astype(BF16)
-    own = mm(coarse_low, jnp.concatenate([tiles_ref[h] for h in range(highs)], axis=1), NT)
-    first = near_ref.shape[0] - highs * count
-    theirs = jnp.concatenate([near_ref[first + h * count : first + (h + 1) * count, :] for h in range(highs)], axis=1)
-    other = mm(coarse_low, theirs, NT)
+    coarse_low = jnp.concatenate(
+        [jnp.concatenate([total[rows * h : rows * (h + 1)] for h in range(i, highs, 2)], axis=1) for i in range(2)], axis=0
+    ).astype(BF16)
+    tiles = jnp.concatenate([tiles_ref[p] for p in range(pairs)], axis=0)
+    theirs = near_ref[near_ref.shape[0] - pairs * LANES :, :]
+    both = mm(coarse_low, jnp.concatenate([tiles, theirs], axis=1))
+    own = both[:rows, :count] + both[rows:, count : 2 * count]
+    other = both[:rows, 2 * count : 3 * count] + both[rows:, 3 * count :]
     odd = lax.rem(lax.axis_index("wide"), 2) == 1
     chunk = jnp.concatenate([jnp.where(odd, other, own), jnp.where(odd, own, other)], axis=1).astype(BF16)
     for at in range(send_ref.shape[0]):
@@ -276,20 +284,26 @@
         copy.start()
         copies.append(copy)
 
-    cuts = piece(0, half // 2) + piece(half // 2, half // 2)
-    send(cuts[1])
-    send(cuts[2])
-    for side, (start, _, exists) in enumerate(sides(width)):
+    faces = []
+    for side, (_, _, exists) in enumerate(sides(width)):
         rest, shift = rests[side], shifts[side * loads : (side + 1) * loads]
-        scale = 1.0 / rest[loads * pieces : loads * pieces + pieces]
+        weights = jnp.concatenate([rest[loads * pieces + q : loads * pieces + q + 1] for q in range(pieces)], axis=1)
+        scale = 1.0 / weights
         if exists is not None:
             scale = jnp.where(exists, scale, 0.0)
-        for q in range(pieces):
-            face = (rest[q * loads : (q + 1) * loads] + shift[:, q * LANES : (q + 1) * LANES]) * scale[q : q + 1]
-            at = pl.ds(pl.multiple_of(start + q * LANES, LANES), LANES)
-            out_ref[:, at] = out_ref[:, at] + face
-    send(cuts[0])
-    send(cuts[3])
+        inside = jnp.concatenate([rest[q * loads : (q + 1) * loads] for q in range(pieces)], axis=1)
+        faces.append((inside + shift) * scale)
+    odd = lax.rem(lax.axis_index("wide"), 2) == 1
+    from_below, from_above = jnp.where(odd, faces[0], faces[1]), jnp.where(odd, faces[1], faces[0])
+
+    one, two = piece(0, half // 2)
+    out_ref[:, :NF] = out_ref[:, :NF] + from_below
+    send(one)
+    send(two)
+    one, two = piece(half // 2, half // 2)
+    send(one)
+    out_ref[:, width - NF :] = out_ref[:, width - NF :] + from_above
+    send(two)
     for copy in copies:
         copy.wait()
 
@@ -314,7 +328,7 @@
     wide, narrow = lax.axis_size("wide"), lax.axis_size("narrow")
     mult = mult.reshape(1, width)
 
-    pieces = 4
+    pieces = 3
     hbm = pl.BlockSpec(memory_space=pltpu.HBM)
 
     def pinned(*arrays):
@@ -347,12 +361,16 @@
         functools.partial(interior_kernel, spans=spans),
         out_shape=(
             jax.ShapeDtypeStruct((loads, width), BF16),
-            jax.ShapeDtypeStruct((highs, coarse_inv.shape[0], LANES), BF16),
+            jax.ShapeDtypeStruct((highs // 2, LANES, LANES), BF16),
         ),
         input_output_aliases={0: 0},
         in_specs=[VMEM, hbm, hbm],
         out_specs=(VMEM, VMEM),
-        scratch_shapes=[pltpu.VMEM(dirichlet_inv.shape, BF16), pltpu.SemaphoreType.DMA((len(spans) + highs,))],
+        scratch_shapes=[
+            pltpu.VMEM(dirichlet_inv.shape, BF16),
+            pltpu.VMEM(coarse_inv.shape, BF16),
+            pltpu.SemaphoreType.DMA((len(spans) + 1,)),
+        ],
         compiler_params=params(),
         cost_estimate=pl.CostEstimate(flops=2 * 16 * blocks * size * size, bytes_accessed=2 * blocks * size * size, transcendentals=0),
         name="interior",
@@ -380,6 +398,7 @@
     far = lax.ppermute(far, "wide", [(i, (((i + 1) ^ 1) - 1) % wide) for i in range(wide)])
     near = lax.ppermute(near, "wide", [(i, i ^ 1) for i in range(wide)])
     packets = lax.all_to_all(send, "wide", 0, 0)
+    packets, near, far = lax.optimization_barrier((packets, near, far))
 
     send, hot, owner = pl.pallas_call(
         functools.partial(coarse_kernel, width=width),
@@ -393,7 +412,6 @@
         compiler_params=params(),
         name="coarse",
     )(packets, tiles, coarse_index, near)
-    send, near, far = lax.optimization_barrier((send, near, far))
     cores = [[chip * 2 + core for chip in range(wide // 2)] for core in range(2)]
     corr = lax.all_to_all(send, "wide", 0, 0, axis_index_groups=cores)
 

time: 49.1 us -> 49 us (level)
  transfers between devices with their start and end apart: 3 -> 3, of which waited for: 1 -> 1; matrix products, arithmetic and copies ran while one was open for 0% -> 0% of each run, Pallas kernels for 10% -> 8%
where the time goes in v5:
time: 49 us; the launch traced here: 48.7 us
  blocking collectives  23.4 us (48%)
  starting transfers between devices  12.4 us (25%)
  Pallas kernels  10.1 us (21%)
  waiting for transfers between devices  2.8 us (6%)
    all_to_all x1, blocking collectives, per_device(): packets = lax.all_to_all(send, 'wide', 0, 0)  14.2 us
    all_to_all x1, blocking collectives, per_device(): corr = lax.all_to_all(send, 'wide', 0, 0, axis_index_groups=cores)  9.2 us
    all_to_all x1, starting transfers between devices, per_device(): parts = lax.all_to_all(send, 'narrow', 0, 0)  9.03 us
    pallas_call x1, Pallas kernels, per_device(): pl.pallas_call(functools.partial(interior_kernel, spans=spans), out_shape...  4.03 us
    pallas_call x1, Pallas kernels, per_device(): pl.pallas_call(head_kernel, out_shape=(jax.ShapeDtypeStruct(fine_basis.sh...  2.85 us
    all_to_all x1, waiting for transfers between devices, per_device(): parts = lax.all_to_all(send, 'narrow', 0, 0)  2.79 us
    ppermute x1, starting transfers between devices, per_device(): near = lax.ppermute(near, 'wide', [(i, i ^ 1) for i in range(wide)])  2.18 us
    pallas_call x1, Pallas kernels, per_device(): pl.pallas_call(tail_kernel, out_shape=jax.ShapeDtypeStruct((loads, width)...  1.83 us
  transfers between devices with their start and end apart: 3, of which 1 were waited for; matrix products, arithmetic and copies ran while one was open for 0% of the time, Pallas kernels for 8%

profile of v5, /device:TPU:1, one launch (start us, length us, event | category | flops | bytes accessed | tf_op | source)
XLA Modules:
  0.0 48.7 jit_solution(13048808123288266786)
XLA Ops:
  0.0 2.9 %head.1 = (bf16[9216,128]{1,0:T(8,128)(2,1)S(1)}, bf16[4,9216]{1,0:T(4,128)(2,1)S(1)}, f32[1,9216]{1,0:T(1,128)S(1)}, bf16[8,16,128]{2,1,0:T(8,128)(2,1)}) custom-call(f32[4,9216]{1,0:T(4,128)} %resid_hbm.1, s32[1,9216]{1,0:T(1,128)} %bitcast.1, bf16[9216,128]{1,0:T(8,128)(2,1)} %basis_hbm.1, s32[1,128]{1,0:T(1,128)} %index_ref.1), custom_call_target="tpu_custom_call" | custom-call | tf_op jit(solution)/shard_map/head/pallas_call | solution.py:337
  2.9 9.0 %all-to-all-start = ((bf16[8,16,128]{2,1,0:T(8,128)(2,1)}), bf16[8,16,128]{2,1,0:T(8,128)(2,1)S(1)}, u32[]{:S(2)}, u32[]{:S(2)}) async-start(bf16[8,16,128]{2,1,0:T(8,128)(2,1)} %get-tuple-element.22), calls=%async_computation | async-start | bytes 65536 | tf_op jit(solution)/shard_map/all_to_all | solution.py:356
  11.9 0.0 copy-start
  11.9 0.0 copy-start.1
  11.9 0.0 copy-start.2
  11.9 0.0 copy-start.3
  11.9 4.0 %interior.1 = (bf16[4,9216]{1,0:T(4,128)(2,1)S(1)}, bf16[8,128,128]{2,1,0:T(8,128)(2,1)S(1)}) custom-call(bf16[4,9216]{1,0:T(4,128)(2,1)S(1)} %get-tuple-element.23.weighted_ref, bf16[24,384,384]{2,1,0:T(8,128)(2,1)} %blocks_hbm.1, bf16[64,2048]{1,0:T(8,128)(2,1)} %coarse_inv_hbm.1), custom_call_target="tpu_custom_call", output_to_operand_aliasing={{0}: (0, {})} | custom-call | flops 113246208 | bytes 7077888 | tf_op jit(solution)/shard_map/interior/pallas_call | solution.py:360
  16.0 2.8 %all-to-all-done.parts_ref = bf16[8,16,128]{2,1,0:T(8,128)(2,1)S(1)} async-done(((bf16[8,16,128]{2,1,0:T(8,128)(2,1)}), bf16[8,16,128]{2,1,0:T(8,128)(2,1)S(1)}, u32[]{:S(2)}, u32[]{:S(2)}) %all-to-all-start) | async-done | bytes 32800 | tf_op jit(solution)/shard_map/all_to_all | solution.py:356
  18.8 0.0 copy-done
  18.8 0.0 copy-done.1
  18.8 0.0 copy-done.2
  18.8 0.0 copy-done.3
  18.8 0.6 %level2.1 = (f32[4,128]{1,0:T(4,128)S(1)}, bf16[32,8,128]{2,1,0:T(8,128)(2,1)S(1)}, bf16[128,128]{1,0:T(8,128)(2,1)S(1)}, bf16[2368,128]{1,0:T(8,128)(2,1)S(1)}, bf16[1344,128]{1,0:T(8,128)(2,1)S(1)}) custom-call(bf16[8,16,128]{2,1,0:T(8,128)(2,1)S(1)} %all-to-all-done.parts_ref, bf16[512,512]{1,0:T(8,128)(2,1)S(1)} %copy-done, ...), custom_call_target="tpu_custom_call" | custom-call | tf_op jit(solution)/shard_map/level2/pallas_call | solution.py:380
  19.4 2.2 %collective-permute-start = (bf16[2368,128]{1,0:T(8,128)(2,1)S(1)}, bf16[2368,128]{1,0:T(8,128)(2,1)S(1)}, u32[]{:S(2)}, u32[]{:S(2)}) collective-permute-start(bf16[2368,128]{1,0:T(8,128)(2,1)S(1)} %get-tuple-element.29), channel_id=1, source_target_pairs={{0,8},{8,0},{16,24},{24,16},{32,40},{40,32},{48,56},{56,48},{64,72... | collective-permute-start | bytes 1818632 | tf_op jit(solution)/shard_map/ppermute | solution.py:399
  21.6 1.2 %collective-permute-start.1 = (bf16[1344,128]{1,0:T(8,128)(2,1)S(1)}, bf16[1344,128]{1,0:T(8,128)(2,1)S(1)}, u32[]{:S(2)}, u32[]{:S(2)}) collective-permute-start(bf16[1344,128]{1,0:T(8,128)(2,1)S(1)} %get-tuple-element.30), channel_id=1, source_target_pairs={{0,248},{8,16},{16,8},{24,32},{32,24},{40,48},{48,40},{56,64},{64,... | collective-permute-start | bytes 1032200 | tf_op jit(solution)/shard_map/ppermute | solution.py:398
  22.8 14.2 %all_to_all.15.packets_ref = bf16[32,8,128]{2,1,0:T(8,128)(2,1)S(1)} all-to-all(bf16[32,8,128]{2,1,0:T(8,128)(2,1)S(1)} %get-tuple-element.28), channel_id=1, replica_groups=mesh['wide'=32,'narrow'=8] {'wide'}, dimensions={0} | all-to-all | bytes 131072 | tf_op jit(solution)/shard_map/all_to_all | solution.py:400
  36.9 0.0 collective-permute-done.1.far_ref
  36.9 0.0 collective-permute-done.near_ref
  36.9 0.8 %coarse.1 = (bf16[16,8,128]{2,1,0:T(8,128)(2,1)S(1)}, bf16[128,384]{1,0:T(8,128)(2,1)S(1)}, f32[8,384]{1,0:T(8,128)S(1)}) custom-call(bf16[32,8,128]{2,1,0:T(8,128)(2,1)S(1)} %all_to_all.15.packets_ref, bf16[8,128,128]{2,1,0:T(8,128)(2,1)S(1)} %get-tuple-element.27.tiles_ref, s32[1,128]{1,0:T(1,128)S(1)} %copy-done.2, ...), custom_call_target="tpu_custom_call" | custom-call | tf_op jit(solution)/shard_map/coarse/pallas_call | solution.py:403
  37.7 9.2 %all_to_all.16.corr_ref = bf16[16,8,128]{2,1,0:T(8,128)(2,1)S(1)} all-to-all(bf16[16,8,128]{2,1,0:T(8,128)(2,1)S(1)} %get-tuple-element.33), channel_id=1, replica_groups={{0,16,32,48,64,80,96,112,128,144,160,176,192,208,224,240},{8,24,40,56,7..., dimensions={0} | all-to-all | bytes 65536 | tf_op jit(solution)/shard_map/all_to_all | solution.py:416
  46.9 1.8 %tail.1 = f32[4,9216]{1,0:T(4,128)} custom-call(bf16[16,8,128]{2,1,0:T(8,128)(2,1)S(1)} %all_to_all.16.corr_ref, bf16[128,384]{1,0:T(8,128)(2,1)S(1)} %get-tuple-element.34.hot_ref, f32[8,384]{1,0:T(8,128)S(1)} %get-tuple-element.35.owner_ref, f32[4,128]{1,0:T(4,128)S(1)} %get-tuple-element.36.local_ref, bf16[128,128]{1,0:T(8,128)(2,1)S(1)} %get-tuple-element.37.picked_ref, ...), custom_call_target="tpu_custom_call" | custom-call | tf_op jit(solution)/shard_map/tail/pallas_call | solution.py:418
Async XLA Ops:
  2.9 15.9 %all-to-all-start = ((bf16[8,16,128]{2,1,0:T(8,128)(2,1)}), bf16[8,16,128]{2,1,0:T(8,128)(2,1)S(1)}, u32[]{:S(2)}, u32[]{:S(2)}) async-start(bf16[8,16,128]{2,1,0:T(8,128)(2,1)} %get-tuple-element.22), calls=%async_computation | async-start | bytes 65536 | tf_op jit(solution)/shard_map/all_to_all | solution.py:356
  11.9 6.9 %copy-start = (bf16[512,512]{1,0:T(8,128)(2,1)S(1)}, bf16[512,512]{1,0:T(8,128)(2,1)}, u32[]{:S(2)}) copy-start(bf16[512,512]{1,0:T(8,128)(2,1)} %inverse_ref.1) | copy-start | bytes 1572868
  11.9 6.9 %copy-start.1 = (bf16[512,128]{1,0:T(8,128)(2,1)S(1)}, bf16[512,128]{1,0:T(8,128)(2,1)}, u32[]{:S(2)}) copy-start(bf16[512,128]{1,0:T(8,128)(2,1)} %level2_basis_ref.1) | copy-start | bytes 393220
  11.9 6.9 %copy-start.2 = (s32[1,128]{1,0:T(1,128)S(1)}, s32[1,128]{1,0:T(1,128)}, u32[]{:S(2)}) copy-start(s32[1,128]{1,0:T(1,128)} %coarse_index_ref.3) | copy-start | bytes 1540
  11.9 6.9 %copy-start.3 = (s32[1,128]{1,0:T(1,128)S(1)}, s32[1,128]{1,0:T(1,128)}, u32[]{:S(2)}) copy-start(s32[1,128]{1,0:T(1,128)} %index_ref.1) | copy-start | bytes 1540
  19.4 17.6 %collective-permute-start = (bf16[2368,128]{1,0:T(8,128)(2,1)S(1)}, bf16[2368,128]{1,0:T(8,128)(2,1)S(1)}, u32[]{:S(2)}, u32[]{:S(2)}) collective-permute-start(bf16[2368,128]{1,0:T(8,128)(2,1)S(1)} %get-tuple-element.29), channel_id=1, source_target_pairs={{0,8},{8,0},{16,24},{24,16},{32,40},{40,32},{48,56},{56,48},{64,72... | collective-permute-start | bytes 1818632 | tf_op jit(solution)/shard_map/ppermute | solution.py:399
  21.6 15.4 %collective-permute-start.1 = (bf16[1344,128]{1,0:T(8,128)(2,1)S(1)}, bf16[1344,128]{1,0:T(8,128)(2,1)S(1)}, u32[]{:S(2)}, u32[]{:S(2)}) collective-permute-start(bf16[1344,128]{1,0:T(8,128)(2,1)S(1)} %get-tuple-element.30), channel_id=1, source_target_pairs={{0,248},{8,16},{16,8},{24,32},{32,24},{40,48},{48,40},{56,64},{64,... | collective-permute-start | bytes 1032200 | tf_op jit(solution)/shard_map/ppermute | solution.py:398

commit v6 on v5

--- a/solution.py
+++ b/solution.py
@@ -24,11 +24,11 @@
 
 
 def split_mm(a, b, dims=NN):
-    high = a.astype(BF16)
-    rest = a - high.astype(F32)
-    mid = rest.astype(BF16)
-    low = (rest - mid.astype(F32)).astype(BF16)
-    return mm(high, b, dims) + (mm(mid, b, dims) + mm(low, b, dims))
+    high = a.astype(BF16).astype(F32)
+    mid = (a - high).astype(BF16).astype(F32)
+    parts = mm(jnp.concatenate([high, mid, a - high - mid], axis=0).astype(BF16), b, dims)
+    rows = a.shape[0]
+    return parts[:rows] + (parts[rows : 2 * rows] + parts[2 * rows :])
 
 
 def side_by_side(a, b):
@@ -163,7 +163,7 @@
     low = jnp.concatenate([total[q * loads : (q + 1) * loads] for q in range(total.shape[0] // loads)], axis=1).astype(BF16)
     local = mm(low, inverse_ref[...], NT)
     select = selector(index_ref[...], level2_basis_ref.shape[0])
-    chosen = mm(select, level2_basis_ref[...]).astype(BF16)
+    chosen = jnp.transpose(mm(select, level2_basis_ref[...])).astype(BF16)
     picked_ref[...] = chosen
     local_picked = split_mm(local, select, NT)
     local_ref[...] = local_picked
@@ -260,24 +260,22 @@
     for c in range(chips):
         picked += jnp.where(owner == float(c), picks[rows * c : rows * (c + 1)], 0.0)
     picked = picked.astype(BF16)
-    gathered = local_ref[...] + mm(picked[:, :LANES], picked_ref[...], NT)[:loads]
+    gathered = local_ref[...] + mm(picked[:, :LANES], picked_ref[...])[:loads]
     gathered = side_by_side(gathered, gathered)
     theirs, rests = [], []
     for side, face_ref in enumerate((near_ref, far_ref)):
         lanes = slice((side + 1) * LANES, (side + 2) * LANES)
         rest = face_ref[NF + LANES : NF + LANES + REST, :].astype(F32)
-        theirs.append(rest[LOCAL : LOCAL + loads] + mm(picked[:, lanes], face_ref[NF : NF + LANES, :], NT)[:loads])
+        theirs.append(rest[LOCAL : LOCAL + loads] + mm(picked[:, lanes], face_ref[NF : NF + LANES, :])[:loads])
         rests.append(rest)
     shifts = mm(side_by_side(*theirs), jnp.concatenate([near_ref[:NF, :], far_ref[:NF, :]], axis=1), NT)
 
     copies = []
 
-    def piece(at, count):
-        one, two = slice(at, at + count), slice(half + at, half + at + count)
+    def piece(one, two):
         shift = mm(gathered, jnp.concatenate([basis_ref[one, :], basis_ref[two, :]], axis=1), NT)
         out_ref[:, one] = (interior_ref[:, one].astype(F32) + shift[:loads]) * inverse_ref[:, one]
         out_ref[:, two] = (interior_ref[:, two].astype(F32) + shift[loads:]) * inverse_ref[:, two]
-        return one, two
 
     def send(cut):
         copy = pltpu.make_async_copy(out_ref.at[:, cut], out_hbm.at[:, cut], sems.at[len(copies)])
@@ -296,14 +294,17 @@
     odd = lax.rem(lax.axis_index("wide"), 2) == 1
     from_below, from_above = jnp.where(odd, faces[0], faces[1]), jnp.where(odd, faces[1], faces[0])
 
-    one, two = piece(0, half // 2)
+    quarter = width // 4
+    ends = slice(0, quarter), slice(width - quarter, width)
+    piece(*ends)
     out_ref[:, :NF] = out_ref[:, :NF] + from_below
-    send(one)
-    send(two)
-    one, two = piece(half // 2, half // 2)
-    send(one)
     out_ref[:, width - NF :] = out_ref[:, width - NF :] + from_above
-    send(two)
+    send(ends[0])
+    send(ends[1])
+    middle = slice(quarter, half), slice(half, width - quarter)
+    piece(*middle)
+    send(middle[0])
+    send(middle[1])
     for copy in copies:
         copy.wait()
 

time: 49 us -> 48.8 us (level)
  no operation moved by 1% of the time
where the time goes in v6:
time: 48.8 us; the launch traced here: 48.6 us
  blocking collectives  23.4 us (48%)
  starting transfers between devices  12.4 us (25%)
  Pallas kernels  9.9 us (20%)
  waiting for transfers between devices  2.8 us (6%)
    all_to_all x1, blocking collectives, per_device(): packets = lax.all_to_all(send, 'wide', 0, 0)  14.2 us
    all_to_all x1, blocking collectives, per_device(): corr = lax.all_to_all(send, 'wide', 0, 0, axis_index_groups=cores)  9.19 us
    all_to_all x1, starting transfers between devices, per_device(): parts = lax.all_to_all(send, 'narrow', 0, 0)  9.03 us
    pallas_call x1, Pallas kernels, per_device(): pl.pallas_call(functools.partial(interior_kernel, spans=spans), out_shape...  4.03 us
    pallas_call x1, Pallas kernels, per_device(): pl.pallas_call(head_kernel, out_shape=(jax.ShapeDtypeStruct(fine_basis.sh...  2.83 us
    all_to_all x1, waiting for transfers between devices, per_device(): parts = lax.all_to_all(send, 'narrow', 0, 0)  2.79 us
    ppermute x1, starting transfers between devices, per_device(): near = lax.ppermute(near, 'wide', [(i, i ^ 1) for i in range(wide)])  2.19 us
    pallas_call x1, Pallas kernels, per_device(): pl.pallas_call(tail_kernel, out_shape=jax.ShapeDtypeStruct((loads, width)...  1.81 us
  transfers between devices with their start and end apart: 3, of which 1 were waited for; matrix products, arithmetic and copies ran while one was open for 0% of the time, Pallas kernels for 8%

profile of v6, /device:TPU:1, one launch (start us, length us, event | category | flops | bytes accessed | tf_op | source)
XLA Modules:
  0.0 48.6 jit_solution(17057949513495919535)
XLA Ops:
  0.0 2.8 %head.1 = (bf16[9216,128]{1,0:T(8,128)(2,1)S(1)}, bf16[4,9216]{1,0:T(4,128)(2,1)S(1)}, f32[1,9216]{1,0:T(1,128)S(1)}, bf16[8,16,128]{2,1,0:T(8,128)(2,1)}) custom-call(f32[4,9216]{1,0:T(4,128)} %resid_hbm.1, s32[1,9216]{1,0:T(1,128)} %bitcast.1, bf16[9216,128]{1,0:T(8,128)(2,1)} %basis_hbm.1, s32[1,128]{1,0:T(1,128)} %index_ref.1), custom_call_target="tpu_custom_call" | custom-call | tf_op jit(solution)/shard_map/head/pallas_call | solution.py:338
  2.8 9.0 %all-to-all-start = ((bf16[8,16,128]{2,1,0:T(8,128)(2,1)}), bf16[8,16,128]{2,1,0:T(8,128)(2,1)S(1)}, u32[]{:S(2)}, u32[]{:S(2)}) async-start(bf16[8,16,128]{2,1,0:T(8,128)(2,1)} %get-tuple-element.22), calls=%async_computation | async-start | bytes 65536 | tf_op jit(solution)/shard_map/all_to_all | solution.py:357
  11.9 0.0 copy-start
  11.9 0.0 copy-start.1
  11.9 0.0 copy-start.2
  11.9 0.0 copy-start.3
  11.9 4.0 %interior.1 = (bf16[4,9216]{1,0:T(4,128)(2,1)S(1)}, bf16[8,128,128]{2,1,0:T(8,128)(2,1)S(1)}) custom-call(bf16[4,9216]{1,0:T(4,128)(2,1)S(1)} %get-tuple-element.23.weighted_ref, bf16[24,384,384]{2,1,0:T(8,128)(2,1)} %blocks_hbm.1, bf16[64,2048]{1,0:T(8,128)(2,1)} %coarse_inv_hbm.1), custom_call_target="tpu_custom_call", output_to_operand_aliasing={{0}: (0, {})} | custom-call | flops 113246208 | bytes 7077888 | tf_op jit(solution)/shard_map/interior/pallas_call | solution.py:361
  15.9 2.8 %all-to-all-done.parts_ref = bf16[8,16,128]{2,1,0:T(8,128)(2,1)S(1)} async-done(((bf16[8,16,128]{2,1,0:T(8,128)(2,1)}), bf16[8,16,128]{2,1,0:T(8,128)(2,1)S(1)}, u32[]{:S(2)}, u32[]{:S(2)}) %all-to-all-start) | async-done | bytes 32800 | tf_op jit(solution)/shard_map/all_to_all | solution.py:357
  18.7 0.0 copy-done
  18.7 0.0 copy-done.1
  18.7 0.0 copy-done.2
  18.8 0.0 copy-done.3
  18.8 0.4 level2.1
  19.2 2.2 %collective-permute-start = (bf16[2368,128]{1,0:T(8,128)(2,1)S(1)}, bf16[2368,128]{1,0:T(8,128)(2,1)S(1)}, u32[]{:S(2)}, u32[]{:S(2)}) collective-permute-start(bf16[2368,128]{1,0:T(8,128)(2,1)S(1)} %get-tuple-element.29), channel_id=1, source_target_pairs={{0,8},{8,0},{16,24},{24,16},{32,40},{40,32},{48,56},{56,48},{64,72... | collective-permute-start | bytes 1818632 | tf_op jit(solution)/shard_map/ppermute | solution.py:400
  21.4 1.2 %collective-permute-start.1 = (bf16[1344,128]{1,0:T(8,128)(2,1)S(1)}, bf16[1344,128]{1,0:T(8,128)(2,1)S(1)}, u32[]{:S(2)}, u32[]{:S(2)}) collective-permute-start(bf16[1344,128]{1,0:T(8,128)(2,1)S(1)} %get-tuple-element.30), channel_id=1, source_target_pairs={{0,248},{8,16},{16,8},{24,32},{32,24},{40,48},{48,40},{56,64},{64,... | collective-permute-start | bytes 1032200 | tf_op jit(solution)/shard_map/ppermute | solution.py:399
  22.6 14.2 %all_to_all.15.packets_ref = bf16[32,8,128]{2,1,0:T(8,128)(2,1)S(1)} all-to-all(bf16[32,8,128]{2,1,0:T(8,128)(2,1)S(1)} %get-tuple-element.28), channel_id=1, replica_groups=mesh['wide'=32,'narrow'=8] {'wide'}, dimensions={0} | all-to-all | bytes 131072 | tf_op jit(solution)/shard_map/all_to_all | solution.py:401
  36.8 0.0 collective-permute-done.1.far_ref
  36.8 0.0 collective-permute-done.near_ref
  36.8 0.8 %coarse.1 = (bf16[16,8,128]{2,1,0:T(8,128)(2,1)S(1)}, bf16[128,384]{1,0:T(8,128)(2,1)S(1)}, f32[8,384]{1,0:T(8,128)S(1)}) custom-call(bf16[32,8,128]{2,1,0:T(8,128)(2,1)S(1)} %all_to_all.15.packets_ref, bf16[8,128,128]{2,1,0:T(8,128)(2,1)S(1)} %get-tuple-element.27.tiles_ref, s32[1,128]{1,0:T(1,128)S(1)} %copy-done.2, ...), custom_call_target="tpu_custom_call" | custom-call | tf_op jit(solution)/shard_map/coarse/pallas_call | solution.py:404
  37.6 9.2 %all_to_all.16.corr_ref = bf16[16,8,128]{2,1,0:T(8,128)(2,1)S(1)} all-to-all(bf16[16,8,128]{2,1,0:T(8,128)(2,1)S(1)} %get-tuple-element.33), channel_id=1, replica_groups={{0,16,32,48,64,80,96,112,128,144,160,176,192,208,224,240},{8,24,40,56,7..., dimensions={0} | all-to-all | bytes 65536 | tf_op jit(solution)/shard_map/all_to_all | solution.py:417
  46.7 1.8 %tail.1 = f32[4,9216]{1,0:T(4,128)} custom-call(bf16[16,8,128]{2,1,0:T(8,128)(2,1)S(1)} %all_to_all.16.corr_ref, bf16[128,384]{1,0:T(8,128)(2,1)S(1)} %get-tuple-element.34.hot_ref, f32[8,384]{1,0:T(8,128)S(1)} %get-tuple-element.35.owner_ref, f32[4,128]{1,0:T(4,128)S(1)} %get-tuple-element.36.local_ref, bf16[128,128]{1,0:T(8,128)(2,1)S(1)} %get-tuple-element.37.picked_ref, ...), custom_call_target="tpu_custom_call" | custom-call | tf_op jit(solution)/shard_map/tail/pallas_call | solution.py:419
Async XLA Ops:
  2.8 15.9 %all-to-all-start = ((bf16[8,16,128]{2,1,0:T(8,128)(2,1)}), bf16[8,16,128]{2,1,0:T(8,128)(2,1)S(1)}, u32[]{:S(2)}, u32[]{:S(2)}) async-start(bf16[8,16,128]{2,1,0:T(8,128)(2,1)} %get-tuple-element.22), calls=%async_computation | async-start | bytes 65536 | tf_op jit(solution)/shard_map/all_to_all | solution.py:357
  11.9 6.9 %copy-start = (bf16[512,512]{1,0:T(8,128)(2,1)S(1)}, bf16[512,512]{1,0:T(8,128)(2,1)}, u32[]{:S(2)}) copy-start(bf16[512,512]{1,0:T(8,128)(2,1)} %inverse_ref.1) | copy-start | bytes 1572868
  11.9 6.9 %copy-start.1 = (bf16[512,128]{1,0:T(8,128)(2,1)S(1)}, bf16[512,128]{1,0:T(8,128)(2,1)}, u32[]{:S(2)}) copy-start(bf16[512,128]{1,0:T(8,128)(2,1)} %level2_basis_ref.1) | copy-start | bytes 393220
  11.9 6.9 %copy-start.2 = (s32[1,128]{1,0:T(1,128)S(1)}, s32[1,128]{1,0:T(1,128)}, u32[]{:S(2)}) copy-start(s32[1,128]{1,0:T(1,128)} %coarse_index_ref.3) | copy-start | bytes 1540
  11.9 6.9 %copy-start.3 = (s32[1,128]{1,0:T(1,128)S(1)}, s32[1,128]{1,0:T(1,128)}, u32[]{:S(2)}) copy-start(s32[1,128]{1,0:T(1,128)} %index_ref.1) | copy-start | bytes 1540
  19.2 17.6 %collective-permute-start = (bf16[2368,128]{1,0:T(8,128)(2,1)S(1)}, bf16[2368,128]{1,0:T(8,128)(2,1)S(1)}, u32[]{:S(2)}, u32[]{:S(2)}) collective-permute-start(bf16[2368,128]{1,0:T(8,128)(2,1)S(1)} %get-tuple-element.29), channel_id=1, source_target_pairs={{0,8},{8,0},{16,24},{24,16},{32,40},{40,32},{48,56},{56,48},{64,72... | collective-permute-start | bytes 1818632 | tf_op jit(solution)/shard_map/ppermute | solution.py:400
  21.4 15.4 %collective-permute-start.1 = (bf16[1344,128]{1,0:T(8,128)(2,1)S(1)}, bf16[1344,128]{1,0:T(8,128)(2,1)S(1)}, u32[]{:S(2)}, u32[]{:S(2)}) collective-permute-start(bf16[1344,128]{1,0:T(8,128)(2,1)S(1)} %get-tuple-element.30), channel_id=1, source_target_pairs={{0,248},{8,16},{16,8},{24,32},{32,24},{40,48},{48,40},{56,64},{64,... | collective-permute-start | bytes 1032200 | tf_op jit(solution)/shard_map/ppermute | solution.py:399

commit v7 on v6

--- a/solution.py
+++ b/solution.py
@@ -220,7 +220,7 @@
     own = both[:rows, :count] + both[rows:, count : 2 * count]
     other = both[:rows, 2 * count : 3 * count] + both[rows:, 3 * count :]
     odd = lax.rem(lax.axis_index("wide"), 2) == 1
-    chunk = jnp.concatenate([jnp.where(odd, other, own), jnp.where(odd, own, other)], axis=1).astype(BF16)
+    chunk = jnp.concatenate([jnp.where(odd, other, own), jnp.where(odd, own, other)], axis=1)[:loads].astype(BF16)
     for at in range(send_ref.shape[0]):
         send_ref[at] = chunk
 
@@ -252,14 +252,15 @@
     loads, width = interior_ref.shape
     half = width // 2
     pieces = NF // LANES
-    chips, rows = corr_ref.shape[0], corr_ref.shape[1]
+    chips = corr_ref.shape[0]
     table = jnp.concatenate([corr_ref[c].astype(F32) for c in range(chips)], axis=0).astype(BF16)
     picks = mm(table, hot_ref[...])
     owner = owner_ref[...]
+    owner = owner - jnp.where(lax.broadcasted_iota(jnp.int32, owner.shape, 0) >= loads, 1.0, 0.0)
     picked = jnp.zeros(owner.shape, F32)
-    for c in range(chips):
-        picked += jnp.where(owner == float(c), picks[rows * c : rows * (c + 1)], 0.0)
-    picked = picked.astype(BF16)
+    for c in range(0, chips, 2):
+        picked += jnp.where(owner == float(c), picks[loads * c : loads * (c + 2)], 0.0)
+    picked = (picked[:loads] + picked[loads:]).astype(BF16)
     gathered = local_ref[...] + mm(picked[:, :LANES], picked_ref[...])[:loads]
     gathered = side_by_side(gathered, gathered)
     theirs, rests = [], []
@@ -301,10 +302,8 @@
     out_ref[:, width - NF :] = out_ref[:, width - NF :] + from_above
     send(ends[0])
     send(ends[1])
-    middle = slice(quarter, half), slice(half, width - quarter)
-    piece(*middle)
-    send(middle[0])
-    send(middle[1])
+    piece(slice(quarter, half), slice(half, width - quarter))
+    send(slice(quarter, width - quarter))
     for copy in copies:
         copy.wait()
 
@@ -404,7 +403,7 @@
     send, hot, owner = pl.pallas_call(
         functools.partial(coarse_kernel, width=width),
         out_shape=(
-            jax.ShapeDtypeStruct((wide // 2, 8, LANES), BF16),
+            jax.ShapeDtypeStruct((wide // 2, loads, LANES), BF16),
             jax.ShapeDtypeStruct((LANES, 3 * LANES), BF16),
             jax.ShapeDtypeStruct((8, 3 * LANES), F32),
         ),
@@ -421,7 +420,7 @@
         out_shape=jax.ShapeDtypeStruct((loads, width), F32),
         in_specs=[VMEM] * 10,
         out_specs=hbm,
-        scratch_shapes=[pltpu.VMEM((loads, width), F32), pltpu.SemaphoreType.DMA((4,))],
+        scratch_shapes=[pltpu.VMEM((loads, width), F32), pltpu.SemaphoreType.DMA((3,))],
         compiler_params=params(),
         name="tail",
     )(corr, hot, owner, local, chosen, near, far, interior, inverse, basis)

time: 48.8 us -> 48.8 us (level)
  no operation moved by 1% of the time
where the time goes in v7:
time: 48.8 us; the launch traced here: 48.5 us
  blocking collectives  23.3 us (48%)
  starting transfers between devices  12.4 us (25%)
  Pallas kernels  9.89 us (20%)
  waiting for transfers between devices  2.8 us (6%)
    all_to_all x1, blocking collectives, per_device(): packets = lax.all_to_all(send, 'wide', 0, 0)  14.2 us
    all_to_all x1, blocking collectives, per_device(): corr = lax.all_to_all(send, 'wide', 0, 0, axis_index_groups=cores)  9.17 us
    all_to_all x1, starting transfers between devices, per_device(): parts = lax.all_to_all(send, 'narrow', 0, 0)  9.03 us
    pallas_call x1, Pallas kernels, per_device(): pl.pallas_call(functools.partial(interior_kernel, spans=spans), out_shape...  4.03 us
    pallas_call x1, Pallas kernels, per_device(): pl.pallas_call(head_kernel, out_shape=(jax.ShapeDtypeStruct(fine_basis.sh...  2.83 us
    all_to_all x1, waiting for transfers between devices, per_device(): parts = lax.all_to_all(send, 'narrow', 0, 0)  2.79 us
    ppermute x1, starting transfers between devices, per_device(): near = lax.ppermute(near, 'wide', [(i, i ^ 1) for i in range(wide)])  2.19 us
    pallas_call x1, Pallas kernels, per_device(): pl.pallas_call(tail_kernel, out_shape=jax.ShapeDtypeStruct((loads, width)...  1.79 us
  transfers between devices with their start and end apart: 3, of which 1 were waited for; matrix products, arithmetic and copies ran while one was open for 0% of the time, Pallas kernels for 8%

profile of v7, /device:TPU:1, one launch (start us, length us, event | category | flops | bytes accessed | tf_op | source)
XLA Modules:
  0.0 48.5 jit_solution(9168545567992981733)
XLA Ops:
  0.0 2.8 %head.1 = (bf16[9216,128]{1,0:T(8,128)(2,1)S(1)}, bf16[4,9216]{1,0:T(4,128)(2,1)S(1)}, f32[1,9216]{1,0:T(1,128)S(1)}, bf16[8,16,128]{2,1,0:T(8,128)(2,1)}) custom-call(f32[4,9216]{1,0:T(4,128)} %resid_hbm.1, s32[1,9216]{1,0:T(1,128)} %bitcast.1, bf16[9216,128]{1,0:T(8,128)(2,1)} %basis_hbm.1, s32[1,128]{1,0:T(1,128)} %index_ref.1), custom_call_target="tpu_custom_call" | custom-call | tf_op jit(solution)/shard_map/head/pallas_call | solution.py:337
  2.8 9.0 %all-to-all-start = ((bf16[8,16,128]{2,1,0:T(8,128)(2,1)}), bf16[8,16,128]{2,1,0:T(8,128)(2,1)S(1)}, u32[]{:S(2)}, u32[]{:S(2)}) async-start(bf16[8,16,128]{2,1,0:T(8,128)(2,1)} %get-tuple-element.22), calls=%async_computation | async-start | bytes 65536 | tf_op jit(solution)/shard_map/all_to_all | solution.py:356
  11.9 0.0 copy-start
  11.9 0.0 copy-start.1
  11.9 0.0 copy-start.2
  11.9 0.0 copy-start.3
  11.9 4.0 %interior.1 = (bf16[4,9216]{1,0:T(4,128)(2,1)S(1)}, bf16[8,128,128]{2,1,0:T(8,128)(2,1)S(1)}) custom-call(bf16[4,9216]{1,0:T(4,128)(2,1)S(1)} %get-tuple-element.23.weighted_ref, bf16[24,384,384]{2,1,0:T(8,128)(2,1)} %blocks_hbm.1, bf16[64,2048]{1,0:T(8,128)(2,1)} %coarse_inv_hbm.1), custom_call_target="tpu_custom_call", output_to_operand_aliasing={{0}: (0, {})} | custom-call | flops 113246208 | bytes 7077888 | tf_op jit(solution)/shard_map/interior/pallas_call | solution.py:360
  15.9 2.8 %all-to-all-done.parts_ref = bf16[8,16,128]{2,1,0:T(8,128)(2,1)S(1)} async-done(((bf16[8,16,128]{2,1,0:T(8,128)(2,1)}), bf16[8,16,128]{2,1,0:T(8,128)(2,1)S(1)}, u32[]{:S(2)}, u32[]{:S(2)}) %all-to-all-start) | async-done | bytes 32800 | tf_op jit(solution)/shard_map/all_to_all | solution.py:356
  18.7 0.0 copy-done
  18.7 0.0 copy-done.1
  18.7 0.0 copy-done.2
  18.8 0.0 copy-done.3
  18.8 0.4 level2.1
  19.2 2.2 %collective-permute-start = (bf16[2368,128]{1,0:T(8,128)(2,1)S(1)}, bf16[2368,128]{1,0:T(8,128)(2,1)S(1)}, u32[]{:S(2)}, u32[]{:S(2)}) collective-permute-start(bf16[2368,128]{1,0:T(8,128)(2,1)S(1)} %get-tuple-element.29), channel_id=1, source_target_pairs={{0,8},{8,0},{16,24},{24,16},{32,40},{40,32},{48,56},{56,48},{64,72... | collective-permute-start | bytes 1818632 | tf_op jit(solution)/shard_map/ppermute | solution.py:399
  21.4 1.2 %collective-permute-start.1 = (bf16[1344,128]{1,0:T(8,128)(2,1)S(1)}, bf16[1344,128]{1,0:T(8,128)(2,1)S(1)}, u32[]{:S(2)}, u32[]{:S(2)}) collective-permute-start(bf16[1344,128]{1,0:T(8,128)(2,1)S(1)} %get-tuple-element.30), channel_id=1, source_target_pairs={{0,248},{8,16},{16,8},{24,32},{32,24},{40,48},{48,40},{56,64},{64,... | collective-permute-start | bytes 1032200 | tf_op jit(solution)/shard_map/ppermute | solution.py:398
  22.6 14.2 %all_to_all.15.packets_ref = bf16[32,8,128]{2,1,0:T(8,128)(2,1)S(1)} all-to-all(bf16[32,8,128]{2,1,0:T(8,128)(2,1)S(1)} %get-tuple-element.28), channel_id=1, replica_groups=mesh['wide'=32,'narrow'=8] {'wide'}, dimensions={0} | all-to-all | bytes 131072 | tf_op jit(solution)/shard_map/all_to_all | solution.py:400
  36.8 0.0 collective-permute-done.1.far_ref
  36.8 0.0 collective-permute-done.near_ref
  36.8 0.8 %coarse.1 = (bf16[16,4,128]{2,1,0:T(4,128)(2,1)S(1)}, bf16[128,384]{1,0:T(8,128)(2,1)S(1)}, f32[8,384]{1,0:T(8,128)S(1)}) custom-call(bf16[32,8,128]{2,1,0:T(8,128)(2,1)S(1)} %all_to_all.15.packets_ref, bf16[8,128,128]{2,1,0:T(8,128)(2,1)S(1)} %get-tuple-element.27.tiles_ref, s32[1,128]{1,0:T(1,128)S(1)} %copy-done.2, ...), custom_call_target="tpu_custom_call" | custom-call | tf_op jit(solution)/shard_map/coarse/pallas_call | solution.py:403
  37.6 9.2 %all_to_all.16.corr_ref = bf16[16,4,128]{2,1,0:T(4,128)(2,1)S(1)} all-to-all(bf16[16,4,128]{2,1,0:T(4,128)(2,1)S(1)} %get-tuple-element.33), channel_id=1, replica_groups={{0,16,32,48,64,80,96,112,128,144,160,176,192,208,224,240},{8,24,40,56,7..., dimensions={0} | all-to-all | bytes 32768 | tf_op jit(solution)/shard_map/all_to_all | solution.py:416
  46.7 1.8 %tail.1 = f32[4,9216]{1,0:T(4,128)} custom-call(bf16[16,4,128]{2,1,0:T(4,128)(2,1)S(1)} %all_to_all.16.corr_ref, bf16[128,384]{1,0:T(8,128)(2,1)S(1)} %get-tuple-element.34.hot_ref, f32[8,384]{1,0:T(8,128)S(1)} %get-tuple-element.35.owner_ref, f32[4,128]{1,0:T(4,128)S(1)} %get-tuple-element.36.local_ref, bf16[128,128]{1,0:T(8,128)(2,1)S(1)} %get-tuple-element.37.picked_ref, ...), custom_call_target="tpu_custom_call" | custom-call | tf_op jit(solution)/shard_map/tail/pallas_call | solution.py:418
Async XLA Ops:
  2.8 15.9 %all-to-all-start = ((bf16[8,16,128]{2,1,0:T(8,128)(2,1)}), bf16[8,16,128]{2,1,0:T(8,128)(2,1)S(1)}, u32[]{:S(2)}, u32[]{:S(2)}) async-start(bf16[8,16,128]{2,1,0:T(8,128)(2,1)} %get-tuple-element.22), calls=%async_computation | async-start | bytes 65536 | tf_op jit(solution)/shard_map/all_to_all | solution.py:356
  11.9 6.9 %copy-start = (bf16[512,512]{1,0:T(8,128)(2,1)S(1)}, bf16[512,512]{1,0:T(8,128)(2,1)}, u32[]{:S(2)}) copy-start(bf16[512,512]{1,0:T(8,128)(2,1)} %inverse_ref.1) | copy-start | bytes 1572868
  11.9 6.9 %copy-start.1 = (bf16[512,128]{1,0:T(8,128)(2,1)S(1)}, bf16[512,128]{1,0:T(8,128)(2,1)}, u32[]{:S(2)}) copy-start(bf16[512,128]{1,0:T(8,128)(2,1)} %level2_basis_ref.1) | copy-start | bytes 393220
  11.9 6.9 %copy-start.2 = (s32[1,128]{1,0:T(1,128)S(1)}, s32[1,128]{1,0:T(1,128)}, u32[]{:S(2)}) copy-start(s32[1,128]{1,0:T(1,128)} %coarse_index_ref.3) | copy-start | bytes 1540
  11.9 6.9 %copy-start.3 = (s32[1,128]{1,0:T(1,128)S(1)}, s32[1,128]{1,0:T(1,128)}, u32[]{:S(2)}) copy-start(s32[1,128]{1,0:T(1,128)} %index_ref.1) | copy-start | bytes 1540
  19.2 17.6 %collective-permute-start = (bf16[2368,128]{1,0:T(8,128)(2,1)S(1)}, bf16[2368,128]{1,0:T(8,128)(2,1)S(1)}, u32[]{:S(2)}, u32[]{:S(2)}) collective-permute-start(bf16[2368,128]{1,0:T(8,128)(2,1)S(1)} %get-tuple-element.29), channel_id=1, source_target_pairs={{0,8},{8,0},{16,24},{24,16},{32,40},{40,32},{48,56},{56,48},{64,72... | collective-permute-start | bytes 1818632 | tf_op jit(solution)/shard_map/ppermute | solution.py:399
  21.4 15.4 %collective-permute-start.1 = (bf16[1344,128]{1,0:T(8,128)(2,1)S(1)}, bf16[1344,128]{1,0:T(8,128)(2,1)S(1)}, u32[]{:S(2)}, u32[]{:S(2)}) collective-permute-start(bf16[1344,128]{1,0:T(8,128)(2,1)S(1)} %get-tuple-element.30), channel_id=1, source_target_pairs={{0,248},{8,16},{16,8},{24,32},{32,24},{40,48},{48,40},{56,64},{64,... | collective-permute-start | bytes 1032200 | tf_op jit(solution)/shard_map/ppermute | solution.py:398

commit v8 on v7

--- a/solution.py
+++ b/solution.py
@@ -195,32 +195,32 @@
 
 def coarse_kernel(packets_ref, tiles_ref, coarse_index_ref, near_ref, send_ref, hot_ref, owner_ref, *, width):
     loads = 4
-    groups, rows = packets_ref.shape[0], packets_ref.shape[1]
+    groups = packets_ref.shape[0]
     pairs = tiles_ref.shape[0]
     highs, count = 2 * pairs, tiles_ref.shape[2] // 2
     row = lax.broadcasted_iota(jnp.int32, (LANES, LANES), 0).astype(F32).astype(BF16)
+    which = jnp.concatenate([jnp.full((loads, LANES), float(i), F32) for i in range(4)], axis=0)
     tall, hot = [], []
     for g in range(groups):
         packet = packets_ref[g].astype(F32)
-        twice = jnp.concatenate([packet, packet], axis=0).astype(BF16)
-        high = jnp.broadcast_to(packet[loads : loads + 1], (2 * rows, LANES))
-        which = jnp.concatenate([jnp.zeros((rows, LANES), F32), jnp.ones((rows, LANES), F32)], axis=0)
+        four = jnp.concatenate([packet[:loads]] * 4, axis=0).astype(BF16)
+        high = jnp.broadcast_to(packet[loads : loads + 1], (4 * loads, LANES))
         high = (high - which).astype(BF16)
         low = jnp.broadcast_to(packet[loads + 1 : loads + 2], (LANES, LANES)).astype(BF16)
         zero, one = jnp.zeros((), BF16), jnp.ones((), BF16)
-        tall.append(jnp.concatenate([jnp.where(high == jnp.asarray(h, BF16), twice, zero) for h in range(0, highs, 2)], axis=0))
+        tall.append(jnp.concatenate([jnp.where(high == jnp.asarray(h, BF16), four, zero) for h in range(0, highs, 4)], axis=0))
         hot.append(jnp.where(row == low, one, zero))
     total = mm(jnp.concatenate(tall, axis=1), jnp.concatenate(hot, axis=1), NT)
     coarse_low = jnp.concatenate(
-        [jnp.concatenate([total[rows * h : rows * (h + 1)] for h in range(i, highs, 2)], axis=1) for i in range(2)], axis=0
+        [jnp.concatenate([total[loads * h : loads * (h + 1)] for h in range(i, highs, 2)], axis=1) for i in range(2)], axis=0
     ).astype(BF16)
     tiles = jnp.concatenate([tiles_ref[p] for p in range(pairs)], axis=0)
     theirs = near_ref[near_ref.shape[0] - pairs * LANES :, :]
     both = mm(coarse_low, jnp.concatenate([tiles, theirs], axis=1))
-    own = both[:rows, :count] + both[rows:, count : 2 * count]
-    other = both[:rows, 2 * count : 3 * count] + both[rows:, 3 * count :]
+    own = both[:loads, :count] + both[loads:, count : 2 * count]
+    other = both[:loads, 2 * count : 3 * count] + both[loads:, 3 * count :]
     odd = lax.rem(lax.axis_index("wide"), 2) == 1
-    chunk = jnp.concatenate([jnp.where(odd, other, own), jnp.where(odd, own, other)], axis=1)[:loads].astype(BF16)
+    chunk = jnp.concatenate([jnp.where(odd, other, own), jnp.where(odd, own, other)], axis=1).astype(BF16)
     for at in range(send_ref.shape[0]):
         send_ref[at] = chunk
 

time: 48.8 us -> 48.8 us (level)
  no operation moved by 1% of the time
where the time goes in v8:
time: 48.8 us; the launch traced here: 48.6 us
  blocking collectives  23.3 us (48%)
  starting transfers between devices  12.4 us (25%)
  Pallas kernels  9.99 us (20%)
  waiting for transfers between devices  2.8 us (6%)
    all_to_all x1, blocking collectives, per_device(): packets = lax.all_to_all(send, 'wide', 0, 0)  14.2 us
    all_to_all x1, blocking collectives, per_device(): corr = lax.all_to_all(send, 'wide', 0, 0, axis_index_groups=cores)  9.13 us
    all_to_all x1, starting transfers between devices, per_device(): parts = lax.all_to_all(send, 'narrow', 0, 0)  9.03 us
    pallas_call x1, Pallas kernels, per_device(): pl.pallas_call(functools.partial(interior_kernel, spans=spans), out_shape...  4.03 us
    pallas_call x1, Pallas kernels, per_device(): pl.pallas_call(head_kernel, out_shape=(jax.ShapeDtypeStruct(fine_basis.sh...  2.83 us
    all_to_all x1, waiting for transfers between devices, per_device(): parts = lax.all_to_all(send, 'narrow', 0, 0)  2.79 us
    ppermute x1, starting transfers between devices, per_device(): near = lax.ppermute(near, 'wide', [(i, i ^ 1) for i in range(wide)])  2.19 us
    pallas_call x1, Pallas kernels, per_device(): pl.pallas_call(tail_kernel, out_shape=jax.ShapeDtypeStruct((loads, width)...  1.79 us
  transfers between devices with their start and end apart: 3, of which 1 were waited for; matrix products, arithmetic and copies ran while one was open for 0% of the time, Pallas kernels for 8%

profile of v8, /device:TPU:1, one launch (start us, length us, event | category | flops | bytes accessed | tf_op | source)
XLA Modules:
  0.0 48.6 jit_solution(16027736867996519235)
XLA Ops:
  0.0 2.8 %head.1 = (bf16[9216,128]{1,0:T(8,128)(2,1)S(1)}, bf16[4,9216]{1,0:T(4,128)(2,1)S(1)}, f32[1,9216]{1,0:T(1,128)S(1)}, bf16[8,16,128]{2,1,0:T(8,128)(2,1)}) custom-call(f32[4,9216]{1,0:T(4,128)} %resid_hbm.1, s32[1,9216]{1,0:T(1,128)} %bitcast.1, bf16[9216,128]{1,0:T(8,128)(2,1)} %basis_hbm.1, s32[1,128]{1,0:T(1,128)} %index_ref.1), custom_call_target="tpu_custom_call" | custom-call | tf_op jit(solution)/shard_map/head/pallas_call | solution.py:337
  2.8 9.0 %all-to-all-start = ((bf16[8,16,128]{2,1,0:T(8,128)(2,1)}), bf16[8,16,128]{2,1,0:T(8,128)(2,1)S(1)}, u32[]{:S(2)}, u32[]{:S(2)}) async-start(bf16[8,16,128]{2,1,0:T(8,128)(2,1)} %get-tuple-element.22), calls=%async_computation | async-start | bytes 65536 | tf_op jit(solution)/shard_map/all_to_all | solution.py:356
  11.9 0.0 copy-start
  11.9 0.0 copy-start.1
  11.9 0.0 copy-start.2
  11.9 0.0 copy-start.3
  11.9 4.0 %interior.1 = (bf16[4,9216]{1,0:T(4,128)(2,1)S(1)}, bf16[8,128,128]{2,1,0:T(8,128)(2,1)S(1)}) custom-call(bf16[4,9216]{1,0:T(4,128)(2,1)S(1)} %get-tuple-element.23.weighted_ref, bf16[24,384,384]{2,1,0:T(8,128)(2,1)} %blocks_hbm.1, bf16[64,2048]{1,0:T(8,128)(2,1)} %coarse_inv_hbm.1), custom_call_target="tpu_custom_call", output_to_operand_aliasing={{0}: (0, {})} | custom-call | flops 113246208 | bytes 7077888 | tf_op jit(solution)/shard_map/interior/pallas_call | solution.py:360
  15.9 2.8 %all-to-all-done.parts_ref = bf16[8,16,128]{2,1,0:T(8,128)(2,1)S(1)} async-done(((bf16[8,16,128]{2,1,0:T(8,128)(2,1)}), bf16[8,16,128]{2,1,0:T(8,128)(2,1)S(1)}, u32[]{:S(2)}, u32[]{:S(2)}) %all-to-all-start) | async-done | bytes 32800 | tf_op jit(solution)/shard_map/all_to_all | solution.py:356
  18.7 0.0 copy-done
  18.7 0.0 copy-done.1
  18.7 0.0 copy-done.2
  18.8 0.0 copy-done.3
  18.8 0.4 level2.1
  19.2 2.2 %collective-permute-start = (bf16[2368,128]{1,0:T(8,128)(2,1)S(1)}, bf16[2368,128]{1,0:T(8,128)(2,1)S(1)}, u32[]{:S(2)}, u32[]{:S(2)}) collective-permute-start(bf16[2368,128]{1,0:T(8,128)(2,1)S(1)} %get-tuple-element.29), channel_id=1, source_target_pairs={{0,8},{8,0},{16,24},{24,16},{32,40},{40,32},{48,56},{56,48},{64,72... | collective-permute-start | bytes 1818632 | tf_op jit(solution)/shard_map/ppermute | solution.py:399
  21.4 1.2 %collective-permute-start.1 = (bf16[1344,128]{1,0:T(8,128)(2,1)S(1)}, bf16[1344,128]{1,0:T(8,128)(2,1)S(1)}, u32[]{:S(2)}, u32[]{:S(2)}) collective-permute-start(bf16[1344,128]{1,0:T(8,128)(2,1)S(1)} %get-tuple-element.30), channel_id=1, source_target_pairs={{0,248},{8,16},{16,8},{24,32},{32,24},{40,48},{48,40},{56,64},{64,... | collective-permute-start | bytes 1032200 | tf_op jit(solution)/shard_map/ppermute | solution.py:398
  22.6 14.2 %all_to_all.15.packets_ref = bf16[32,8,128]{2,1,0:T(8,128)(2,1)S(1)} all-to-all(bf16[32,8,128]{2,1,0:T(8,128)(2,1)S(1)} %get-tuple-element.28), channel_id=1, replica_groups=mesh['wide'=32,'narrow'=8] {'wide'}, dimensions={0} | all-to-all | bytes 131072 | tf_op jit(solution)/shard_map/all_to_all | solution.py:400
  36.8 0.0 collective-permute-done.1.far_ref
  36.8 0.0 collective-permute-done.near_ref
  36.8 0.9 %coarse.1 = (bf16[16,4,128]{2,1,0:T(4,128)(2,1)S(1)}, bf16[128,384]{1,0:T(8,128)(2,1)S(1)}, f32[8,384]{1,0:T(8,128)S(1)}) custom-call(bf16[32,8,128]{2,1,0:T(8,128)(2,1)S(1)} %all_to_all.15.packets_ref, bf16[8,128,128]{2,1,0:T(8,128)(2,1)S(1)} %get-tuple-element.27.tiles_ref, s32[1,128]{1,0:T(1,128)S(1)} %copy-done.2, ...), custom_call_target="tpu_custom_call" | custom-call | tf_op jit(solution)/shard_map/coarse/pallas_call | solution.py:403
  37.7 9.1 %all_to_all.16.corr_ref = bf16[16,4,128]{2,1,0:T(4,128)(2,1)S(1)} all-to-all(bf16[16,4,128]{2,1,0:T(4,128)(2,1)S(1)} %get-tuple-element.33), channel_id=1, replica_groups={{0,16,32,48,64,80,96,112,128,144,160,176,192,208,224,240},{8,24,40,56,7..., dimensions={0} | all-to-all | bytes 32768 | tf_op jit(solution)/shard_map/all_to_all | solution.py:416
  46.8 1.8 %tail.1 = f32[4,9216]{1,0:T(4,128)} custom-call(bf16[16,4,128]{2,1,0:T(4,128)(2,1)S(1)} %all_to_all.16.corr_ref, bf16[128,384]{1,0:T(8,128)(2,1)S(1)} %get-tuple-element.34.hot_ref, f32[8,384]{1,0:T(8,128)S(1)} %get-tuple-element.35.owner_ref, f32[4,128]{1,0:T(4,128)S(1)} %get-tuple-element.36.local_ref, bf16[128,128]{1,0:T(8,128)(2,1)S(1)} %get-tuple-element.37.picked_ref, ...), custom_call_target="tpu_custom_call" | custom-call | tf_op jit(solution)/shard_map/tail/pallas_call | solution.py:418
Async XLA Ops:
  2.8 15.9 %all-to-all-start = ((bf16[8,16,128]{2,1,0:T(8,128)(2,1)}), bf16[8,16,128]{2,1,0:T(8,128)(2,1)S(1)}, u32[]{:S(2)}, u32[]{:S(2)}) async-start(bf16[8,16,128]{2,1,0:T(8,128)(2,1)} %get-tuple-element.22), calls=%async_computation | async-start | bytes 65536 | tf_op jit(solution)/shard_map/all_to_all | solution.py:356
  11.9 6.9 %copy-start = (bf16[512,512]{1,0:T(8,128)(2,1)S(1)}, bf16[512,512]{1,0:T(8,128)(2,1)}, u32[]{:S(2)}) copy-start(bf16[512,512]{1,0:T(8,128)(2,1)} %inverse_ref.1) | copy-start | bytes 1572868
  11.9 6.9 %copy-start.1 = (bf16[512,128]{1,0:T(8,128)(2,1)S(1)}, bf16[512,128]{1,0:T(8,128)(2,1)}, u32[]{:S(2)}) copy-start(bf16[512,128]{1,0:T(8,128)(2,1)} %level2_basis_ref.1) | copy-start | bytes 393220
  11.9 6.9 %copy-start.2 = (s32[1,128]{1,0:T(1,128)S(1)}, s32[1,128]{1,0:T(1,128)}, u32[]{:S(2)}) copy-start(s32[1,128]{1,0:T(1,128)} %coarse_index_ref.3) | copy-start | bytes 1540
  11.9 6.9 %copy-start.3 = (s32[1,128]{1,0:T(1,128)S(1)}, s32[1,128]{1,0:T(1,128)}, u32[]{:S(2)}) copy-start(s32[1,128]{1,0:T(1,128)} %index_ref.1) | copy-start | bytes 1540
  19.2 17.6 %collective-permute-start = (bf16[2368,128]{1,0:T(8,128)(2,1)S(1)}, bf16[2368,128]{1,0:T(8,128)(2,1)S(1)}, u32[]{:S(2)}, u32[]{:S(2)}) collective-permute-start(bf16[2368,128]{1,0:T(8,128)(2,1)S(1)} %get-tuple-element.29), channel_id=1, source_target_pairs={{0,8},{8,0},{16,24},{24,16},{32,40},{40,32},{48,56},{56,48},{64,72... | collective-permute-start | bytes 1818632 | tf_op jit(solution)/shard_map/ppermute | solution.py:399
  21.4 15.4 %collective-permute-start.1 = (bf16[1344,128]{1,0:T(8,128)(2,1)S(1)}, bf16[1344,128]{1,0:T(8,128)(2,1)S(1)}, u32[]{:S(2)}, u32[]{:S(2)}) collective-permute-start(bf16[1344,128]{1,0:T(8,128)(2,1)S(1)} %get-tuple-element.30), channel_id=1, source_target_pairs={{0,248},{8,16},{16,8},{24,32},{32,24},{40,48},{48,40},{56,64},{64,... | collective-permute-start | bytes 1032200 | tf_op jit(solution)/shard_map/ppermute | solution.py:398
